TPU v7x, 512 devices: a whole 4x8x8 slice. The times are simulated.
512 devices in a mesh: dp: 16 (over z, core), tp: 32 (over x, y).
Axes of the slice: x: 4, y: 8, z: 8, core: 2. Of those that a mesh axis runs over, the one named last changes fastest.
Arguments:
- queries: bfloat16 [4096, 36864], P(('dp', 'tp')), parts along dimension 0
- cache_latent: bfloat16 [131072, 576], P(('dp', 'tp')), parts along dimension 0
- row_counts: int32 [512], P(('dp', 'tp')), parts along dimension 0, may hold values from 4 to 8, as said below
- row_kinds: int32 [4096], P(('dp', 'tp')), parts along dimension 0, may hold values from 0 to 1
- cache_lengths: int32 [4096], P(('dp', 'tp')), parts along dimension 0, may hold values from 1 to 128
- positions: int32 [4096], P(('dp', 'tp')), parts along dimension 0, may hold values from 0 to 127
- hidden_units: bfloat16 [4096, 9216], P('dp', 'tp'), parts along dimension 0, may hold values from -6 to 6
- down_proj: bfloat16 [9216, 3584], P('tp'), may hold values from -0.0625 to 0.0625
Outputs:
- attended: bfloat16 [4096, 32768], P(('dp', 'tp')), parts along dimension 0
- ffn_out: bfloat16 [4096, 3584], P(('dp', 'tp')), parts along dimension 0
There are 16 independent parts, one for each index of `dp`. A program takes and returns all parts, laid end to end along the dimension named above; an argument that names none is the same for every part. Nothing has to cross between parts.
Inputs may be any that keep to these rules, and one draw needn't show every extreme that they name: `row_counts`: every device has at least 4 live rows; some device has all 8 slots live.
All inputs are finite; a program needn't handle non-finite values.
Results may differ from a plain program's by a relative error of at most 0.02.
Values may be sent and summed in bfloat16 or wider, within the bound.
No kernel may reach another device: no remote copies, remote signals or barrier semaphores. Data moves between devices by JAX's collectives and lax.ppermute only.
A program may use at most 64 MiB of HBM per device.

v0:
```python
import jax
import jax.numpy as jnp
from jax import lax
from jax.sharding import PartitionSpec as P

HEADS = 64
KVL = 512
QK_DIM = 192
LAT = 576


def attend_local(queries, cache_latent, lengths, offsets, kinds, alive):
    row_total = queries.shape[0]
    entries = cache_latent.shape[0]
    scale = QK_DIM ** (-0.5)
    query_rows = queries.reshape(row_total, HEADS, LAT)
    scores = (
        jnp.einsum("rhd,kd->rhk", query_rows, cache_latent, preferred_element_type=jnp.float32)
        * scale
    )
    index = lax.broadcasted_iota(jnp.int32, (1, entries), 1)
    top_entry = (lengths + offsets)[:, None]
    causal = index <= top_entry
    verify = (index < lengths[:, None]) | (index == top_entry)
    allowed = jnp.where(kinds[:, None] == 1, verify, causal)[:, None, :]
    masked = jnp.where(allowed, scores, jnp.float32(-1e30))
    peak = jnp.max(masked, axis=-1, keepdims=True)
    expo = jnp.where(allowed, jnp.exp(masked - peak), jnp.float32(0.0))
    probs = (expo / jnp.sum(expo, axis=-1, keepdims=True)).astype(jnp.bfloat16)
    output = jnp.einsum(
        "rhk,kd->rhd", probs, cache_latent[:, :KVL], preferred_element_type=jnp.float32
    )
    output = jnp.where(alive[:, None, None], output, jnp.float32(0.0))
    return output.astype(jnp.bfloat16).reshape(row_total, HEADS * KVL)


def shards(
    queries, cache_latent, row_counts, row_kinds, cache_lengths, positions, hidden_units, down_proj
):
    row_total = queries.shape[0]
    alive = lax.broadcasted_iota(jnp.int32, (row_total,), 0) < row_counts[0]
    attended = attend_local(queries, cache_latent, cache_lengths, positions, row_kinds, alive)
    all_counts = lax.all_gather(row_counts, "tp", axis=0, tiled=True)
    groups = all_counts.shape[0]
    width_units = hidden_units.shape[1]
    grouped = hidden_units.reshape(groups, row_total, width_units)
    slots = lax.broadcasted_iota(jnp.int32, (groups, row_total), 1)
    live_all = slots < all_counts[:, None]
    masked = jnp.where(live_all[:, :, None], grouped, jnp.zeros_like(grouped)).reshape(
        groups * row_total, width_units
    )
    partial_value = jnp.dot(masked, down_proj, preferred_element_type=jnp.float32)
    summed = lax.psum_scatter(
        partial_value.astype(jnp.bfloat16), "tp", scatter_dimension=0, tiled=True
    )
    return (attended, summed)


def solution(mesh):
    placed = (
        P(("dp", "tp"), None),
        P(("dp", "tp"), None),
        P(("dp", "tp")),
        P(("dp", "tp")),
        P(("dp", "tp")),
        P(("dp", "tp")),
        P("dp", "tp"),
        P("tp", None),
    )
    return jax.shard_map(
        shards,
        mesh=mesh,
        in_specs=placed,
        out_specs=(P(("dp", "tp"), None), P(("dp", "tp"), None)),
        check_vma=False,
    )
```

profile of v0, /device:TPU:16, one launch (start us, length us, event | category | flops | bytes accessed | tf_op | source)
XLA Modules:
  0.0 261.9 jit_solution(17989236124566246082)
XLA Ops:
  7.2 0.0 copy-start
  7.2 0.0 reduce-scatter.2.cloned.1.call-start
  8.0 1.3 dynamic-slice
  9.3 0.8 dynamic-update-slice
  10.0 21.0 %all-reduce = s32[32]{0:T(128)S(1)} all-reduce(s32[32]{0:T(128)S(1)} %dynamic-update-slice), channel_id=1, replica_groups=mesh['dp'=16,'tp'=32] {'tp'}, use_global_device_ids=true, to_apply=%add | all-reduce | flops 32 | bytes 256
  31.1 0.1 iota_compare_fusion
  31.1 0.1 lt.55
  31.2 0.0 copy-done
  31.3 0.0 copy-start.1
  31.3 3.4 %convolution_convert_fusion = bf16[256,3584]{1,0:T(8,128)(2,1)} fusion(bf16[288,3584]{1,0:T(8,128)(2,1)S(1)} %copy-done, bf16[256,288]{0,1:T(8,128)(2,1)} %param.14, pred[256]{0:T(512)(128)(4,1)S(1)} %lt.55), kind=kOutput, calls=%fused_computation.1 | convolution fusion | flops 529473536 | bytes 4047104 | tf_op jit(solution)/shard_map/dot_general | solution.py:52
  34.6 0.0 copy-start.2
  34.6 0.0 copy-start.4
  34.6 0.0 copy-start.5
  34.6 0.0 reduce-scatter.2.cloned.1.call-update
  34.7 0.0 copy-done.1
  34.7 0.8 reshape.100
  35.5 0.0 copy-done.2
  35.5 0.0 copy-done.4
  35.5 0.0 copy-start.3
  35.5 0.0 copy-done.5
  35.6 0.1 fusion.15
  35.6 2.2 fusion.17
  37.9 0.0 copy-done.3
  37.9 1.4 fusion.3
  39.3 1.1 copy.13
  40.4 214.7 %reduce-scatter.2.cloned.1.call-done = bf16[8,3584]{1,0:T(8,128)(2,1)} async-done(((bf16[256,3584]{1,0:T(8,128)(2,1)}), bf16[8,3584]{1,0:T(8,128)(2,1)}) %reduce-scatter.2.cloned.1.call-update) | async-done | bytes 57360 | tf_op jit(solution)/shard_map/reduce_scatter | solution.py:53
  (4 shorter events, 0.0 us)
Async XLA Ops:
  7.2 24.1 %copy-start = (bf16[288,3584]{1,0:T(8,128)(2,1)S(1)}, bf16[288,3584]{1,0:T(8,128)(2,1)}, u32[]{:S(2)}) copy-start(bf16[288,3584]{1,0:T(8,128)(2,1)} %param.15) | copy-start | bytes 6193156
  7.2 247.8 %reduce-scatter.2.cloned.1.call-start = ((), (), s32[]{:S(2)}) async-start(), calls=%async_computation.1 | async-start | bytes 1892352 | tf_op jit(solution)/shard_map/reduce_scatter | solution.py:53
  31.3 3.4 %copy-start.1 = (bf16[8,36864]{1,0:T(8,128)(2,1)S(1)}, bf16[8,36864]{1,0:T(8,128)(2,1)}, u32[]{:S(2)}) copy-start(bf16[8,36864]{1,0:T(8,128)(2,1)} %param.8) | copy-start | bytes 1769476
  34.6 0.9 copy-start.2
  34.6 0.9 copy-start.4
  34.6 0.9 copy-start.5
  35.5 2.4 copy-start.3
Sparse Core Ops, SparseCore 0:
  34.8 220.1 reduce-scatter.1
where the time goes:
time: 262 us
  waiting for transfers between devices  215 us (82%)
  blocking collectives  21 us (8%)
  between operations  14.9 us (6%)
  matrix products  6.99 us (3%)
  local copies, waits for them, and re-layouts  4.04 us (2%)
    reduce_scatter x1, waiting for transfers between devices, shards(): lax.psum_scatter(partial_value.astype(jnp.bfloat16), 'tp', scatter_dimens...  215 us
    unnamed x1, blocking collectives  21 us
  transfers between devices with their start and end apart: 1, of which 1 were waited for; matrix products, arithmetic and copies ran while one was open for 2% of the time, Pallas kernels for 0%

commit v1 on v0

--- a/solution.py
+++ b/solution.py
@@ -7,6 +7,8 @@
 KVL = 512
 QK_DIM = 192
 LAT = 576
+X_RING = 4
+Y_RING = 8
 
 
 def attend_local(queries, cache_latent, lengths, offsets, kinds, alive):
@@ -34,29 +36,76 @@
     return output.astype(jnp.bfloat16).reshape(row_total, HEADS * KVL)
 
 
-def shards(
-    queries, cache_latent, row_counts, row_kinds, cache_lengths, positions, hidden_units, down_proj
-):
-    row_total = queries.shape[0]
-    alive = lax.broadcasted_iota(jnp.int32, (row_total,), 0) < row_counts[0]
-    attended = attend_local(queries, cache_latent, cache_lengths, positions, row_kinds, alive)
-    all_counts = lax.all_gather(row_counts, "tp", axis=0, tiled=True)
-    groups = all_counts.shape[0]
-    width_units = hidden_units.shape[1]
-    grouped = hidden_units.reshape(groups, row_total, width_units)
-    slots = lax.broadcasted_iota(jnp.int32, (groups, row_total), 1)
-    live_all = slots < all_counts[:, None]
-    masked = jnp.where(live_all[:, :, None], grouped, jnp.zeros_like(grouped)).reshape(
-        groups * row_total, width_units
-    )
-    partial_value = jnp.dot(masked, down_proj, preferred_element_type=jnp.float32)
-    summed = lax.psum_scatter(
-        partial_value.astype(jnp.bfloat16), "tp", scatter_dimension=0, tiled=True
-    )
-    return (attended, summed)
+def member(block, kind):
+    return 2 * block + ((kind ^ block) & 1)
+
+
+def device(group, x, y):
+    shift = group % 2
+    return group * X_RING * Y_RING + (x + shift) % X_RING * Y_RING + (y + shift) % Y_RING
+
+
+def block_groups(groups):
+    return [
+        [device(g, member(bx, sx), member(by, sy)) for sx in range(2) for sy in range(2)]
+        for g in range(groups)
+        for bx in range(X_RING // 2)
+        for by in range(Y_RING // 2)
+    ]
+
+
+def kind_groups(groups):
+    return [
+        [
+            device(g, member(bx, sx), member(by, sy))
+            for bx in range(X_RING // 2)
+            for by in range(Y_RING // 2)
+        ]
+        for g in range(groups)
+        for sx in range(2)
+        for sy in range(2)
+    ]
+
+
+def row_order(rows, total, shift):
+    index = lax.broadcasted_iota(jnp.int32, (total,), 0)
+    slot, block = index % rows, index // rows
+    sx, sy, bx, by = block // 16, block // 8 % 2, block // 4 % 2, block % 4
+    x, y = member(bx, sx), member(by, sy)
+    return ((x + shift) % X_RING * Y_RING + (y + shift) % Y_RING) * rows + slot
+
+
+def exchange(values, groups):
+    parts = len(groups[0])
+    moved = lax.all_to_all(
+        values, ("dp", "tp"), 0, 0, tiled=True, axis_index_groups=groups
+    ).reshape(parts, values.shape[0] // parts, values.shape[1])
+    return jnp.sum(moved.astype(jnp.float32), axis=0)
 
 
 def solution(mesh):
+    groups = mesh.shape["dp"]
+
+    def shards(
+        queries, cache_latent, row_counts, row_kinds, cache_lengths, positions, hidden_units, down_proj
+    ):
+        row_total = queries.shape[0]
+        alive = lax.broadcasted_iota(jnp.int32, (row_total,), 0) < row_counts[0]
+        attended = attend_local(queries, cache_latent, cache_lengths, positions, row_kinds, alive)
+        total = hidden_units.shape[0]
+        order = row_order(row_total, total, lax.axis_index("dp") % 2)
+        pick = (order[:, None] == lax.broadcasted_iota(jnp.int32, (total, total), 1)).astype(
+            jnp.bfloat16
+        )
+        ordered = jnp.dot(pick, hidden_units, preferred_element_type=jnp.float32).astype(
+            jnp.bfloat16
+        )
+        partial_value = jnp.dot(ordered, down_proj, preferred_element_type=jnp.float32)
+        quarter = exchange(partial_value.astype(jnp.bfloat16), block_groups(groups))
+        summed = exchange(quarter.astype(jnp.bfloat16), kind_groups(groups))
+        summed = jnp.where(alive[:, None], summed, jnp.float32(0.0)).astype(jnp.bfloat16)
+        return (attended, summed)
+
     placed = (
         P(("dp", "tp"), None),
         P(("dp", "tp"), None),

time: 262 us -> 51.7 us (0.20)
  the two profiles are of different devices: /device:TPU:16 before, /device:TPU:334 now
where the time goes in v1:
time: 51.7 us; the launch traced here: 51.3 us
  blocking collectives  17.9 us (35%)
  starting transfers between devices  9.78 us (19%)
  waiting for transfers between devices  8.03 us (16%)
  matrix products  6.1 us (12%)
  local copies, waits for them, and re-layouts  4.48 us (9%)
  other arithmetic  3.62 us (7%)
  between operations  1.37 us (3%)
    all_to_all x1, blocking collectives, exchange(): lax.all_to_all(values, ('dp', 'tp'), 0, 0, tiled=True, axis_index_groups=...  17.9 us
    all_to_all x1, starting transfers between devices, exchange(): lax.all_to_all(values, ('dp', 'tp'), 0, 0, tiled=True, axis_index_groups=...  9.78 us
    all_to_all x1, waiting for transfers between devices, exchange(): lax.all_to_all(values, ('dp', 'tp'), 0, 0, tiled=True, axis_index_groups=...  8.03 us
    dot_general x1, matrix products, shards(): jnp.dot(ordered, down_proj, preferred_element_type=jnp.float32)  3.45 us
    reduce_sum x2, other arithmetic, exchange(): return jnp.sum(moved.astype(jnp.float32), axis=0)  2.79 us
    unnamed x11, local copies, waits for them, and re-layouts  2.63 us
    reshape x1, local copies, waits for them, and re-layouts, attend_local(): query_rows = queries.reshape(row_total, HEADS, LAT)  1.84 us
    dot_general x1, matrix products, attend_local(): jnp.einsum('rhk,kd->rhd', probs, cache_latent[:, :KVL], preferred_element...  1.39 us
  transfers between devices with their start and end apart: 1, of which 1 were waited for; matrix products, arithmetic and copies ran while one was open for 11% of the time, Pallas kernels for 0%

profile of v1, /device:TPU:334, one launch (start us, length us, event | category | flops | bytes accessed | tf_op | source)
XLA Modules:
  0.0 51.3 jit_solution(13480287892345114507)
XLA Ops:
  0.6 0.0 copy-start
  0.7 1.5 %copy-done = bf16[288,3584]{1,0:T(8,128)(2,1)S(1)} copy-done((bf16[288,3584]{1,0:T(8,128)(2,1)S(1)}, bf16[288,3584]{1,0:T(8,128)(2,1)}, u32[]{:S(2)}) %copy-start) | copy-done | bytes 2064408
  2.2 3.5 %convolution_convert_fusion = bf16[256,3584]{1,0:T(8,128)(2,1)} fusion(bf16[288,3584]{1,0:T(8,128)(2,1)S(1)} %copy-done, bf16[256,288]{0,1:T(8,128)(2,1)} %param.14, s32[256]{0:T(256)S(1)} %fusion.17), kind=kOutput, calls=%fused_computation.1 | convolution fusion | flops 567287808 | bytes 4047872 | tf_op jit(solution)/shard_map/dot_general | solution.py:103
  5.7 17.9 %all_to_all.18 = bf16[4,64,3584]{2,1,0:T(8,128)(2,1)} all-to-all(bf16[4,64,3584]{2,1,0:T(8,128)(2,1)} %bitcast.19), channel_id=1, replica_groups={{0,1,8,9},{3,2,11,10},{4,5,12,13},{7,6,15,14},{24,25,16,17},{27,26,19,1..., dimensions={0} | all-to-all | bytes 3670016 | tf_op jit(solution)/shard_map/all_to_all | solution.py:80
  23.6 0.0 copy-start.3
  23.6 0.0 copy-start.1
  23.6 0.0 copy-start.4
  23.6 0.0 copy-start.2
  23.6 2.7 %reduce_sum.31 = bf16[64,3584]{1,0:T(8,128)(2,1)} reduce(bf16[4,64,3584]{2,1,0:T(8,128)(2,1)} %all_to_all.18, bf16[]{:T(256)} %constant.116.clone.1), dimensions={0}, to_apply=%region_2.3 | reduce | flops 688128 | bytes 2293762 | tf_op jit(solution)/shard_map/reduce_sum | solution.py:83
  26.3 9.8 %all-to-all-start.1 = ((bf16[8,8,3584]{2,1,0:T(8,128)(2,1)}), bf16[8,8,3584]{2,1,0:T(8,128)(2,1)S(1)}, u32[]{:S(2)}, u32[]{:S(2)}) async-start(bf16[8,8,3584]{2,1,0:T(8,128)(2,1)} %bitcast.4), calls=%async_computation.1 | async-start | bytes 917504 | tf_op jit(solution)/shard_map/all_to_all | solution.py:80
  36.1 0.0 copy-done.3
  36.8 1.8 %reshape.215 = bf16[8,64,576]{2,1,0:T(8,128)(2,1)S(1)} reshape(bf16[8,36864]{1,0:T(8,128)(2,1)} %param.8) | data formatting | bytes 1179648 | tf_op jit(solution)/shard_map/reshape | solution.py:18
  38.6 0.0 copy-done.1
  38.6 0.0 copy-done.4
  38.7 0.1 fusion.14
  38.7 0.0 copy-done.2
  38.7 1.3 %fusion.25 = (f32[8,64]{1,0:T(8,128)S(1)}, f32[8,64,256]{2,1,0:T(8,128)}) fusion(pred[8,256]{1,0:T(8,128)(4,1)S(1)} %fusion.14, bf16[8,64,576]{2,1,0:T(8,128)(2,1)S(1)} %reshape.215, bf16[256,576]{0,1:T(8,128)(2,1)S(1)} %copy-done.2), kind=kOutput, calls=%fused_computation.65 | convolution fusion | flops 151650560 | bytes 1413120 | tf_op jit(solution)/shard_map/sub | solution.py:30
  40.0 1.4 %fusion.3 = bf16[1,8,64,512]{3,2,1,0:T(8,128)(2,1)S(1)} fusion(pred[8]{0:T(512)(128)(4,1)S(1)} %iota_compare_fusion.6, f32[8,64,256]{2,1,0:T(8,128)} %get-tuple-element.3, bf16[256,576]{0,1:T(8,128)(2,1)S(1)} %copy-done.2, f32[8,64]{1,0:T(8,128)S(1)} %get-tuple-element.2), kind=kOutput, calls=%fused_computation.5 | convolution fusion | flops 135004160 | bytes 1315328 | tf_op jit(solution)/shard_map/rhk,kd->rhd/dot_general | solution.py:32
  41.4 1.1 %copy.13 = bf16[1,8,64,512]{3,1,2,0:T(8,128)(2,1)} copy(bf16[1,8,64,512]{3,2,1,0:T(8,128)(2,1)S(1)} %fusion.3) | data formatting | bytes 1048576
  42.5 8.0 %all-to-all-done.1 = bf16[8,8,3584]{2,1,0:T(8,128)(2,1)S(1)} async-done(((bf16[8,8,3584]{2,1,0:T(8,128)(2,1)}), bf16[8,8,3584]{2,1,0:T(8,128)(2,1)S(1)}, u32[]{:S(2)}, u32[]{:S(2)}) %all-to-all-start.1) | async-done | bytes 458784 | tf_op jit(solution)/shard_map/all_to_all | solution.py:80
  50.5 0.1 convert_reduce_fusion
  50.6 0.7 %select_convert_fusion = bf16[8,3584]{1,0:T(8,128)(2,1)} fusion(bf16[8,3584]{1,0:T(8,128)(2,1)S(1)} %convert_reduce_fusion, pred[8]{0:T(512)(128)(4,1)S(1)} %iota_compare_fusion.6), kind=kLoop, calls=%fused_computation.19 | loop fusion | flops 28672 | bytes 114696 | tf_op jit(solution)/shard_map/convert_element_type | solution.py:106
  (4 shorter events, 0.0 us)
Async XLA Ops:
  0.6 1.6 %copy-start = (bf16[288,3584]{1,0:T(8,128)(2,1)S(1)}, bf16[288,3584]{1,0:T(8,128)(2,1)}, u32[]{:S(2)}) copy-start(bf16[288,3584]{1,0:T(8,128)(2,1)} %param.15) | copy-start | bytes 6193156
  23.6 12.5 %copy-start.3 = (s32[8]{0:T(128)S(1)}, s32[8]{0:T(128)}, u32[]{:S(2)}) copy-start(s32[8]{0:T(128)} %param.11) | copy-start | bytes 100
  23.6 15.0 %copy-start.1 = (s32[8]{0:T(128)S(1)}, s32[8]{0:T(128)}, u32[]{:S(2)}) copy-start(s32[8]{0:T(128)} %param.12) | copy-start | bytes 100
  23.6 15.0 %copy-start.4 = (s32[8]{0:T(128)S(1)}, s32[8]{0:T(128)}, u32[]{:S(2)}) copy-start(s32[8]{0:T(128)} %param.13) | copy-start | bytes 100
  23.6 15.2 %copy-start.2 = (bf16[256,576]{0,1:T(8,128)(2,1)S(1)}, bf16[256,576]{0,1:T(8,128)(2,1)}, u32[]{:S(2)}) copy-start(bf16[256,576]{0,1:T(8,128)(2,1)} %param.9) | copy-start | bytes 884740
  26.3 24.2 %all-to-all-start.1 = ((bf16[8,8,3584]{2,1,0:T(8,128)(2,1)}), bf16[8,8,3584]{2,1,0:T(8,128)(2,1)S(1)}, u32[]{:S(2)}, u32[]{:S(2)}) async-start(bf16[8,8,3584]{2,1,0:T(8,128)(2,1)} %bitcast.4), calls=%async_computation.1 | async-start | bytes 917504 | tf_op jit(solution)/shard_map/all_to_all | solution.py:80

commit v2 on v1

--- a/solution.py
+++ b/solution.py
@@ -1,6 +1,10 @@
+import functools
+
 import jax
 import jax.numpy as jnp
 from jax import lax
+from jax.experimental import pallas as pl
+from jax.experimental.pallas import tpu as pltpu
 from jax.sharding import PartitionSpec as P
 
 HEADS = 64
@@ -9,6 +13,8 @@
 LAT = 576
 X_RING = 4
 Y_RING = 8
+CUTS = (0, 3584)
+TILE = 896
 
 
 def attend_local(queries, cache_latent, lengths, offsets, kinds, alive):
@@ -67,20 +73,113 @@
     ]
 
 
-def row_order(rows, total, shift):
-    index = lax.broadcasted_iota(jnp.int32, (total,), 0)
-    slot, block = index % rows, index // rows
-    sx, sy, bx, by = block // 16, block // 8 % 2, block // 4 % 2, block % 4
+def row_order(index, shift):
+    slot, block = index & 7, index >> 3
+    sx, sy, bx, by = block >> 4, (block >> 3) & 1, (block >> 2) & 1, block & 3
     x, y = member(bx, sx), member(by, sy)
-    return ((x + shift) % X_RING * Y_RING + (y + shift) % Y_RING) * rows + slot
+    return ((((x + shift) & 3) << 3) + ((y + shift) & 7)) * 8 + slot
+
+
+def partial_kernel(tile, shift_ref, units_hbm, down_hbm, out_ref, units, down, sems):
+    tiles = down.shape[0]
+    unit_copy = pltpu.make_async_copy(units_hbm, units, sems.at[tiles])
+    unit_copy.start()
+    copies = [
+        pltpu.make_async_copy(down_hbm.at[:, pl.ds(j * tile, tile)], down.at[j], sems.at[j])
+        for j in range(tiles)
+    ]
+    for copy in copies:
+        copy.start()
+    total = units.shape[1]
+    order = row_order(lax.broadcasted_iota(jnp.int32, (total, total), 0), shift_ref[0])
+    pick = order == lax.broadcasted_iota(jnp.int32, (total, total), 1)
+    pick = jnp.where(pick, 1.0, 0.0).astype(jnp.bfloat16)
+    unit_copy.wait()
+    ordered = lax.dot_general(
+        pick, units[...], (((1,), (1,)), ((), ())), preferred_element_type=jnp.float32
+    ).astype(jnp.bfloat16)
+    for j, copy in enumerate(copies):
+        copy.wait()
+        out_ref[:, pl.ds(j * tile, tile)] = jnp.dot(
+            ordered, down[j], preferred_element_type=jnp.float32
+        ).astype(jnp.bfloat16)
+
+
+def partial_sums(shift, units_t, down_proj):
+    units, total = units_t.shape
+    width = down_proj.shape[1]
+    tiles = width // TILE
+    return pl.pallas_call(
+        functools.partial(partial_kernel, TILE),
+        out_shape=jax.ShapeDtypeStruct((total, width), jnp.bfloat16),
+        in_specs=[
+            pl.BlockSpec(memory_space=pltpu.SMEM),
+            pl.BlockSpec(memory_space=pl.ANY),
+            pl.BlockSpec(memory_space=pl.ANY),
+        ],
+        out_specs=pl.BlockSpec(memory_space=pltpu.VMEM),
+        scratch_shapes=[
+            pltpu.VMEM((units, total), jnp.bfloat16),
+            pltpu.VMEM((tiles, units, TILE), jnp.bfloat16),
+            pltpu.SemaphoreType.DMA((tiles + 1,)),
+        ],
+        compiler_params=pltpu.CompilerParams(vmem_limit_bytes=56 * 2**20),
+        cost_estimate=pl.CostEstimate(
+            flops=2 * total * units * width,
+            bytes_accessed=2 * (units * (width + total) + total * width),
+            transcendentals=0,
+        ),
+        name="partial_sums",
+    )(shift, units_t, down_proj)
+
+
+def sum_kernel(parts, in_ref, out_ref):
+    rows = out_ref.shape[0]
+    value = in_ref[pl.ds(0, rows), :].astype(jnp.float32)
+    for part in range(1, parts):
+        value += in_ref[pl.ds(part * rows, rows), :].astype(jnp.float32)
+    out_ref[...] = value.astype(jnp.bfloat16)
+
+
+def sum_parts(values, parts):
+    rows, width = values.shape[0] // parts, values.shape[1]
+    return pl.pallas_call(
+        functools.partial(sum_kernel, parts),
+        out_shape=jax.ShapeDtypeStruct((rows, width), jnp.bfloat16),
+        compiler_params=pltpu.CompilerParams(vmem_limit_bytes=16 * 2**20),
+        cost_estimate=pl.CostEstimate(
+            flops=values.size, bytes_accessed=2 * (values.size + rows * width), transcendentals=0
+        ),
+        name="sum_parts",
+    )(values)
+
+
+def final_kernel(count_ref, *refs):
+    out_ref = refs[-1]
+    rows = out_ref.shape[0]
+    for (start, stop), ref in zip(zip(CUTS[:-1], CUTS[1:]), refs[:-1]):
+        value = jnp.zeros((rows, stop - start), jnp.float32)
+        for pair in range(0, ref.shape[0], 2 * rows):
+            both = ref[pl.ds(pair, 2 * rows), :].astype(jnp.float32)
+            value += both[:rows] + both[rows:]
+        row = lax.broadcasted_iota(jnp.int32, value.shape, 0)
+        value = jnp.where(row < count_ref[0], value, 0.0)
+        out_ref[:, pl.ds(start, stop - start)] = value.astype(jnp.bfloat16)
+
+
+def final_sum(counts, halves, rows):
+    return pl.pallas_call(
+        final_kernel,
+        out_shape=jax.ShapeDtypeStruct((rows, CUTS[-1]), jnp.bfloat16),
+        in_specs=[pl.BlockSpec(memory_space=pltpu.SMEM)]
+        + [pl.BlockSpec(memory_space=pltpu.VMEM) for _ in halves],
+        compiler_params=pltpu.CompilerParams(vmem_limit_bytes=16 * 2**20),
+        name="final_sum",
+    )(counts, *halves)
 
 
 def exchange(values, groups):
-    parts = len(groups[0])
-    moved = lax.all_to_all(
-        values, ("dp", "tp"), 0, 0, tiled=True, axis_index_groups=groups
-    ).reshape(parts, values.shape[0] // parts, values.shape[1])
-    return jnp.sum(moved.astype(jnp.float32), axis=0)
+    return lax.all_to_all(values, ("dp", "tp"), 0, 0, tiled=True, axis_index_groups=groups)
 
 
 def solution(mesh):
@@ -91,19 +190,14 @@
     ):
         row_total = queries.shape[0]
         alive = lax.broadcasted_iota(jnp.int32, (row_total,), 0) < row_counts[0]
+        shift = (lax.axis_index("dp") % 2).astype(jnp.int32).reshape(1)
+        part = partial_sums(shift, hidden_units.T, down_proj)
+        moved = exchange(part, block_groups(groups))
         attended = attend_local(queries, cache_latent, cache_lengths, positions, row_kinds, alive)
-        total = hidden_units.shape[0]
-        order = row_order(row_total, total, lax.axis_index("dp") % 2)
-        pick = (order[:, None] == lax.broadcasted_iota(jnp.int32, (total, total), 1)).astype(
-            jnp.bfloat16
-        )
-        ordered = jnp.dot(pick, hidden_units, preferred_element_type=jnp.float32).astype(
-            jnp.bfloat16
-        )
-        partial_value = jnp.dot(ordered, down_proj, preferred_element_type=jnp.float32)
-        quarter = exchange(partial_value.astype(jnp.bfloat16), block_groups(groups))
-        summed = exchange(quarter.astype(jnp.bfloat16), kind_groups(groups))
-        summed = jnp.where(alive[:, None], summed, jnp.float32(0.0)).astype(jnp.bfloat16)
+        moved, attended = lax.optimization_barrier((moved, attended))
+        quarter = sum_parts(moved, 4)
+        moved = exchange(quarter, kind_groups(groups))
+        summed = final_sum(row_counts, [moved], row_total)
         return (attended, summed)
 
     placed = (

time: 51.7 us -> 47.1 us (0.911)
  the two profiles are of different devices: /device:TPU:334 before, /device:TPU:200 now
where the time goes in v2:
time: 47.1 us; the launch traced here: 46.8 us
  blocking collectives  23.6 us (50%)
  waiting for transfers between devices  9.44 us (20%)
  Pallas kernels  5.11 us (11%)
  starting transfers between devices  4.36 us (9%)
  local copies, waits for them, and re-layouts  1.92 us (4%)
  between operations  1.41 us (3%)
  matrix products  0.9 us (2%)
    all_to_all x1, blocking collectives, exchange(): lax.all_to_all(values, ('dp', 'tp'), 0, 0, tiled=True, axis_index_groups=...  23.6 us
    all_to_all x1, waiting for transfers between devices, exchange(): lax.all_to_all(values, ('dp', 'tp'), 0, 0, tiled=True, axis_index_groups=...  9.44 us
    all_to_all x1, starting transfers between devices, exchange(): lax.all_to_all(values, ('dp', 'tp'), 0, 0, tiled=True, axis_index_groups=...  4.36 us
    pallas_call x1, Pallas kernels, partial_sums(): pl.pallas_call(functools.partial(partial_kernel, TILE), out_shape=jax.Sha...  4.2 us
    unnamed x11, local copies, waits for them, and re-layouts  1.12 us
  transfers between devices with their start and end apart: 1, of which 1 were waited for; matrix products, arithmetic and copies ran while one was open for 6% of the time, Pallas kernels for 0%

profile of v2, /device:TPU:200, one launch (start us, length us, event | category | flops | bytes accessed | tf_op | source)
XLA Modules:
  0.0 46.8 jit_solution(6969404238464031390)
XLA Ops:
  0.6 4.2 %partial_sums.1 = bf16[256,3584]{1,0:T(8,128)(2,1)} custom-call(s32[1]{0:T(128)} %bitcast.shift_ref, bf16[288,256]{1,0:T(8,128)(2,1)} %bitcast.26, bf16[288,3584]{1,0:T(8,128)(2,1)} %down_hbm.1), custom_call_target="tpu_custom_call" | custom-call | flops 528482304 | bytes 4046848 | tf_op jit(solution)/shard_map/partial_sums/pallas_call | solution.py:112
  4.8 0.0 copy-start
  4.9 0.0 copy-start.1
  4.9 0.0 copy-start.3
  4.9 0.0 copy-start.4
  4.9 0.0 copy-start.2
  4.9 4.4 %all-to-all-start = ((bf16[4,64,3584]{2,1,0:T(8,128)(2,1)}), bf16[4,64,3584]{2,1,0:T(8,128)(2,1)S(1)}, u32[]{:S(2)}, u32[]{:S(2)}) async-start(bf16[4,64,3584]{2,1,0:T(8,128)(2,1)} %bitcast.24), calls=%async_computation | async-start | bytes 3670016 | tf_op jit(solution)/shard_map/all_to_all | solution.py:182
  9.3 0.0 copy-done
  9.3 0.8 %reshape.87 = bf16[8,64,576]{2,1,0:T(8,128)(2,1)S(1)} reshape(bf16[8,36864]{1,0:T(8,128)(2,1)S(1)} %copy-done) | data formatting | bytes 1179648 | tf_op jit(solution)/shard_map/reshape | solution.py:24
  10.7 0.0 copy-done.1
  10.7 0.0 copy-done.3
  10.8 0.0 copy-done.4
  10.8 0.1 fusion.12
  10.9 0.0 copy-done.2
  10.9 0.5 %fusion.13 = (f32[8,64]{1,0:T(8,128)S(1)}, f32[8,64,256]{2,1,0:T(8,128)S(1)}) fusion(pred[8,256]{1,0:T(8,128)(4,1)S(1)} %fusion.12, bf16[8,64,576]{2,1,0:T(8,128)(2,1)S(1)} %reshape.87, bf16[256,576]{0,1:T(8,128)(2,1)S(1)} %copy-done.2), kind=kOutput, calls=%fused_computation.21 | convolution fusion | flops 151650560 | bytes 1413120 | tf_op jit(solution)/shard_map/sub | solution.py:36
  11.4 0.4 fusion.3
  11.8 1.1 %copy.12 = bf16[1,8,64,512]{3,1,2,0:T(8,128)(2,1)} copy(bf16[1,8,64,512]{3,2,1,0:T(8,128)(2,1)S(1)} %fusion.3) | data formatting | bytes 1048576
  12.9 9.4 %all-to-all-done = bf16[4,64,3584]{2,1,0:T(8,128)(2,1)S(1)} async-done(((bf16[4,64,3584]{2,1,0:T(8,128)(2,1)}), bf16[4,64,3584]{2,1,0:T(8,128)(2,1)S(1)}, u32[]{:S(2)}, u32[]{:S(2)}) %all-to-all-start) | async-done | bytes 1835040 | tf_op jit(solution)/shard_map/all_to_all | solution.py:182
  22.3 0.2 sum_parts.1
  22.5 23.6 %all_to_all.23 = bf16[8,8,3584]{2,1,0:T(8,128)(2,1)S(1)} all-to-all(bf16[8,8,3584]{2,1,0:T(8,128)(2,1)S(1)} %bitcast.23), channel_id=1, replica_groups={{0,3,4,7,24,27,28,31},{1,2,5,6,25,26,29,30},{8,11,12,15,16,19,20,23},{9..., dimensions={0} | all-to-all | bytes 917504 | tf_op jit(solution)/shard_map/all_to_all | solution.py:182
  46.2 0.7 %final_sum.1 = bf16[8,3584]{1,0:T(8,128)(2,1)} custom-call(s32[1]{0:T(128)} %copy.13.count_ref, bf16[64,3584]{1,0:T(8,128)(2,1)S(1)} %bitcast.22), custom_call_target="tpu_custom_call" | custom-call | tf_op jit(solution)/shard_map/final_sum/pallas_call | solution.py:171
  (3 shorter events, 0.0 us)
Async XLA Ops:
  4.8 4.4 %copy-start = (bf16[8,36864]{1,0:T(8,128)(2,1)S(1)}, bf16[8,36864]{1,0:T(8,128)(2,1)}, u32[]{:S(2)}) copy-start(bf16[8,36864]{1,0:T(8,128)(2,1)} %param.8) | copy-start | bytes 1769476
  4.9 5.9 %copy-start.1 = (s32[8]{0:T(128)S(1)}, s32[8]{0:T(128)}, u32[]{:S(2)}) copy-start(s32[8]{0:T(128)} %param.12) | copy-start | bytes 100
  4.9 5.9 %copy-start.3 = (s32[8]{0:T(128)S(1)}, s32[8]{0:T(128)}, u32[]{:S(2)}) copy-start(s32[8]{0:T(128)} %param.13) | copy-start | bytes 100
  4.9 5.9 %copy-start.4 = (s32[8]{0:T(128)S(1)}, s32[8]{0:T(128)}, u32[]{:S(2)}) copy-start(s32[8]{0:T(128)} %param.11) | copy-start | bytes 100
  4.9 6.0 %copy-start.2 = (bf16[256,576]{0,1:T(8,128)(2,1)S(1)}, bf16[256,576]{0,1:T(8,128)(2,1)}, u32[]{:S(2)}) copy-start(bf16[256,576]{0,1:T(8,128)(2,1)} %param.9) | copy-start | bytes 884740
  4.9 17.4 %all-to-all-start = ((bf16[4,64,3584]{2,1,0:T(8,128)(2,1)}), bf16[4,64,3584]{2,1,0:T(8,128)(2,1)S(1)}, u32[]{:S(2)}, u32[]{:S(2)}) async-start(bf16[4,64,3584]{2,1,0:T(8,128)(2,1)} %bitcast.24), calls=%async_computation | async-start | bytes 3670016 | tf_op jit(solution)/shard_map/all_to_all | solution.py:182

commit v3 on v2

--- a/solution.py
+++ b/solution.py
@@ -64,8 +64,8 @@
     return [
         [
             device(g, member(bx, sx), member(by, sy))
+            for by in range(Y_RING // 2)
             for bx in range(X_RING // 2)
-            for by in range(Y_RING // 2)
         ]
         for g in range(groups)
         for sx in range(2)
@@ -75,37 +75,42 @@
 
 def row_order(index, shift):
     slot, block = index & 7, index >> 3
-    sx, sy, bx, by = block >> 4, (block >> 3) & 1, (block >> 2) & 1, block & 3
+    sx, sy, bx, by = block >> 4, (block >> 3) & 1, block & 1, (block >> 1) & 3
     x, y = member(bx, sx), member(by, sy)
     return ((((x + shift) & 3) << 3) + ((y + shift) & 7)) * 8 + slot
 
 
-def partial_kernel(tile, shift_ref, units_hbm, down_hbm, out_ref, units, down, sems):
+def partial_kernel(tile, units_hbm, down_hbm, out_hbm, units, down, out, in_sems, out_sems):
     tiles = down.shape[0]
-    unit_copy = pltpu.make_async_copy(units_hbm, units, sems.at[tiles])
+    unit_copy = pltpu.make_async_copy(units_hbm, units, in_sems.at[tiles])
     unit_copy.start()
     copies = [
-        pltpu.make_async_copy(down_hbm.at[:, pl.ds(j * tile, tile)], down.at[j], sems.at[j])
+        pltpu.make_async_copy(down_hbm.at[:, pl.ds(j * tile, tile)], down.at[j], in_sems.at[j])
         for j in range(tiles)
     ]
     for copy in copies:
         copy.start()
     total = units.shape[1]
-    order = row_order(lax.broadcasted_iota(jnp.int32, (total, total), 0), shift_ref[0])
+    shift = lax.axis_index("dp") & 1
+    order = row_order(lax.broadcasted_iota(jnp.int32, (total, total), 0), shift)
     pick = order == lax.broadcasted_iota(jnp.int32, (total, total), 1)
     pick = jnp.where(pick, 1.0, 0.0).astype(jnp.bfloat16)
     unit_copy.wait()
     ordered = lax.dot_general(
         pick, units[...], (((1,), (1,)), ((), ())), preferred_element_type=jnp.float32
     ).astype(jnp.bfloat16)
+    sends = []
     for j, copy in enumerate(copies):
         copy.wait()
-        out_ref[:, pl.ds(j * tile, tile)] = jnp.dot(
-            ordered, down[j], preferred_element_type=jnp.float32
-        ).astype(jnp.bfloat16)
-
-
-def partial_sums(shift, units_t, down_proj):
+        out[j] = jnp.dot(ordered, down[j], preferred_element_type=jnp.float32).astype(jnp.bfloat16)
+        send = pltpu.make_async_copy(out.at[j], out_hbm.at[:, pl.ds(j * tile, tile)], out_sems.at[j])
+        send.start()
+        sends.append(send)
+    for send in sends:
+        send.wait()
+
+
+def partial_sums(units_t, down_proj):
     units, total = units_t.shape
     width = down_proj.shape[1]
     tiles = width // TILE
@@ -113,15 +118,16 @@
         functools.partial(partial_kernel, TILE),
         out_shape=jax.ShapeDtypeStruct((total, width), jnp.bfloat16),
         in_specs=[
-            pl.BlockSpec(memory_space=pltpu.SMEM),
             pl.BlockSpec(memory_space=pl.ANY),
             pl.BlockSpec(memory_space=pl.ANY),
         ],
-        out_specs=pl.BlockSpec(memory_space=pltpu.VMEM),
+        out_specs=pl.BlockSpec(memory_space=pl.ANY),
         scratch_shapes=[
             pltpu.VMEM((units, total), jnp.bfloat16),
             pltpu.VMEM((tiles, units, TILE), jnp.bfloat16),
+            pltpu.VMEM((tiles, total, TILE), jnp.bfloat16),
             pltpu.SemaphoreType.DMA((tiles + 1,)),
+            pltpu.SemaphoreType.DMA((tiles,)),
         ],
         compiler_params=pltpu.CompilerParams(vmem_limit_bytes=56 * 2**20),
         cost_estimate=pl.CostEstimate(
@@ -130,7 +136,7 @@
             transcendentals=0,
         ),
         name="partial_sums",
-    )(shift, units_t, down_proj)
+    )(units_t, down_proj)
 
 
 def sum_kernel(parts, in_ref, out_ref):
@@ -190,8 +196,7 @@
     ):
         row_total = queries.shape[0]
         alive = lax.broadcasted_iota(jnp.int32, (row_total,), 0) < row_counts[0]
-        shift = (lax.axis_index("dp") % 2).astype(jnp.int32).reshape(1)
-        part = partial_sums(shift, hidden_units.T, down_proj)
+        part = partial_sums(hidden_units.T, down_proj)
         moved = exchange(part, block_groups(groups))
         attended = attend_local(queries, cache_latent, cache_lengths, positions, row_kinds, alive)
         moved, attended = lax.optimization_barrier((moved, attended))

time: 47.1 us -> 46.5 us (0.987)
  the two profiles are of different devices: /device:TPU:200 before, /device:TPU:8 now
where the time goes in v3:
time: 46.5 us; the launch traced here: 46.2 us
  blocking collectives  18.2 us (39%)
  starting transfers between devices  9.52 us (20%)
  waiting for transfers between devices  9.43 us (20%)
  Pallas kernels  4.72 us (10%)
  local copies, waits for them, and re-layouts  1.92 us (4%)
  between operations  1.41 us (3%)
  matrix products  0.9 us (2%)
    all_to_all x1, blocking collectives, exchange(): lax.all_to_all(values, ('dp', 'tp'), 0, 0, tiled=True, axis_index_groups=...  18.2 us
    all_to_all x1, starting transfers between devices, exchange(): lax.all_to_all(values, ('dp', 'tp'), 0, 0, tiled=True, axis_index_groups=...  9.52 us
    all_to_all x1, waiting for transfers between devices, exchange(): lax.all_to_all(values, ('dp', 'tp'), 0, 0, tiled=True, axis_index_groups=...  9.43 us
    pallas_call x1, Pallas kernels, partial_sums(): pl.pallas_call(functools.partial(partial_kernel, TILE), out_shape=jax.Sha...  3.81 us
    unnamed x11, local copies, waits for them, and re-layouts  1.12 us
  transfers between devices with their start and end apart: 1, of which 1 were waited for; matrix products, arithmetic and copies ran while one was open for 6% of the time, Pallas kernels for 0%

profile of v3, /device:TPU:8, one launch (start us, length us, event | category | flops | bytes accessed | tf_op | source)
XLA Modules:
  0.0 46.2 jit_solution(12940832792167121880)
XLA Ops:
  0.6 3.8 %partial_sums.1 = bf16[256,3584]{1,0:T(8,128)(2,1)} custom-call(bf16[288,256]{1,0:T(8,128)(2,1)} %bitcast.25, bf16[288,3584]{1,0:T(8,128)(2,1)} %down_hbm.1), custom_call_target="tpu_custom_call" | custom-call | flops 528482304 | bytes 4046848 | tf_op jit(solution)/shard_map/partial_sums/pallas_call | solution.py:117
  4.4 0.0 copy-start
  4.5 0.0 copy-start.1
  4.5 0.0 copy-start.3
  4.5 0.0 copy-start.4
  4.5 0.0 copy-start.2
  4.5 9.5 %all-to-all-start = ((bf16[4,64,3584]{2,1,0:T(8,128)(2,1)}), bf16[4,64,3584]{2,1,0:T(8,128)(2,1)S(1)}, u32[]{:S(2)}, u32[]{:S(2)}) async-start(bf16[4,64,3584]{2,1,0:T(8,128)(2,1)} %bitcast.23), calls=%async_computation | async-start | bytes 3670016 | tf_op jit(solution)/shard_map/all_to_all | solution.py:188
  14.7 0.0 copy-done
  14.7 0.8 %reshape.83 = bf16[8,64,576]{2,1,0:T(8,128)(2,1)S(1)} reshape(bf16[8,36864]{1,0:T(8,128)(2,1)S(1)} %copy-done) | data formatting | bytes 1179648 | tf_op jit(solution)/shard_map/reshape | solution.py:24
  15.5 0.0 copy-done.1
  15.5 0.0 copy-done.3
  15.5 0.0 copy-done.4
  15.6 0.1 fusion.12
  15.6 0.0 copy-done.2
  15.6 0.5 %fusion.13 = (f32[8,64]{1,0:T(8,128)S(1)}, f32[8,64,256]{2,1,0:T(8,128)S(1)}) fusion(pred[8,256]{1,0:T(8,128)(4,1)S(1)} %fusion.12, bf16[8,64,576]{2,1,0:T(8,128)(2,1)S(1)} %reshape.83, bf16[256,576]{0,1:T(8,128)(2,1)S(1)} %copy-done.2), kind=kOutput, calls=%fused_computation.21 | convolution fusion | flops 151650560 | bytes 1413120 | tf_op jit(solution)/shard_map/sub | solution.py:36
  16.2 0.4 fusion.3
  16.6 1.1 %copy.12 = bf16[1,8,64,512]{3,1,2,0:T(8,128)(2,1)} copy(bf16[1,8,64,512]{3,2,1,0:T(8,128)(2,1)S(1)} %fusion.3) | data formatting | bytes 1048576
  17.6 9.4 %all-to-all-done = bf16[4,64,3584]{2,1,0:T(8,128)(2,1)S(1)} async-done(((bf16[4,64,3584]{2,1,0:T(8,128)(2,1)}), bf16[4,64,3584]{2,1,0:T(8,128)(2,1)S(1)}, u32[]{:S(2)}, u32[]{:S(2)}) %all-to-all-start) | async-done | bytes 1835040 | tf_op jit(solution)/shard_map/all_to_all | solution.py:188
  27.1 0.2 sum_parts.1
  27.3 18.2 %all_to_all.23 = bf16[8,8,3584]{2,1,0:T(8,128)(2,1)S(1)} all-to-all(bf16[8,8,3584]{2,1,0:T(8,128)(2,1)S(1)} %bitcast.22), channel_id=1, replica_groups={{0,24,3,27,4,28,7,31},{1,25,2,26,5,29,6,30},{8,16,11,19,12,20,15,23},{9..., dimensions={0} | all-to-all | bytes 917504 | tf_op jit(solution)/shard_map/all_to_all | solution.py:188
  45.5 0.7 %final_sum.1 = bf16[8,3584]{1,0:T(8,128)(2,1)} custom-call(s32[1]{0:T(128)} %copy.13.count_ref, bf16[64,3584]{1,0:T(8,128)(2,1)S(1)} %bitcast.21), custom_call_target="tpu_custom_call" | custom-call | tf_op jit(solution)/shard_map/final_sum/pallas_call | solution.py:177
  (3 shorter events, 0.0 us)
Async XLA Ops:
  4.4 10.2 %copy-start = (bf16[8,36864]{1,0:T(8,128)(2,1)S(1)}, bf16[8,36864]{1,0:T(8,128)(2,1)}, u32[]{:S(2)}) copy-start(bf16[8,36864]{1,0:T(8,128)(2,1)} %param.8) | copy-start | bytes 1769476
  4.5 11.0 %copy-start.1 = (s32[8]{0:T(128)S(1)}, s32[8]{0:T(128)}, u32[]{:S(2)}) copy-start(s32[8]{0:T(128)} %param.12) | copy-start | bytes 100
  4.5 11.0 %copy-start.3 = (s32[8]{0:T(128)S(1)}, s32[8]{0:T(128)}, u32[]{:S(2)}) copy-start(s32[8]{0:T(128)} %param.13) | copy-start | bytes 100
  4.5 11.1 %copy-start.4 = (s32[8]{0:T(128)S(1)}, s32[8]{0:T(128)}, u32[]{:S(2)}) copy-start(s32[8]{0:T(128)} %param.11) | copy-start | bytes 100
  4.5 11.1 %copy-start.2 = (bf16[256,576]{0,1:T(8,128)(2,1)S(1)}, bf16[256,576]{0,1:T(8,128)(2,1)}, u32[]{:S(2)}) copy-start(bf16[256,576]{0,1:T(8,128)(2,1)} %param.9) | copy-start | bytes 884740
  4.5 22.6 %all-to-all-start = ((bf16[4,64,3584]{2,1,0:T(8,128)(2,1)}), bf16[4,64,3584]{2,1,0:T(8,128)(2,1)S(1)}, u32[]{:S(2)}, u32[]{:S(2)}) async-start(bf16[4,64,3584]{2,1,0:T(8,128)(2,1)} %bitcast.23), calls=%async_computation | async-start | bytes 3670016 | tf_op jit(solution)/shard_map/all_to_all | solution.py:188

commit v4 on v3

--- a/solution.py
+++ b/solution.py
@@ -47,13 +47,18 @@
 
 
 def device(group, x, y):
-    shift = group % 2
-    return group * X_RING * Y_RING + (x + shift) % X_RING * Y_RING + (y + shift) % Y_RING
+    core = group % 2
+    return group * X_RING * Y_RING + (x + (1 - core)) % X_RING * Y_RING + (y + (1 - core)) % Y_RING
+
+
+def member_y(block, kind, core):
+    flips = 6 + core * 0
+    return 2 * block + (kind ^ ((flips >> block) & 1))
 
 
 def block_groups(groups):
     return [
-        [device(g, member(bx, sx), member(by, sy)) for sx in range(2) for sy in range(2)]
+        [device(g, member(bx, sx), member_y(by, sy, g % 2)) for sx in range(2) for sy in range(2)]
         for g in range(groups)
         for bx in range(X_RING // 2)
         for by in range(Y_RING // 2)
@@ -63,7 +68,7 @@
 def kind_groups(groups):
     return [
         [
-            device(g, member(bx, sx), member(by, sy))
+            device(g, member(bx, sx), member_y(by, sy, g % 2))
             for by in range(Y_RING // 2)
             for bx in range(X_RING // 2)
         ]
@@ -76,8 +81,8 @@
 def row_order(index, shift):
     slot, block = index & 7, index >> 3
     sx, sy, bx, by = block >> 4, (block >> 3) & 1, block & 1, (block >> 1) & 3
-    x, y = member(bx, sx), member(by, sy)
-    return ((((x + shift) & 3) << 3) + ((y + shift) & 7)) * 8 + slot
+    x, y = member(bx, sx), member_y(by, sy, shift)
+    return ((((x + (1 - shift)) & 3) << 3) + ((y + (1 - shift)) & 7)) * 8 + slot
 
 
 def partial_kernel(tile, units_hbm, down_hbm, out_hbm, units, down, out, in_sems, out_sems):

time: 46.5 us -> 44.8 us (0.963)
  the two profiles are of different devices: /device:TPU:8 before, /device:TPU:12 now
where the time goes in v4:
time: 44.8 us; the launch traced here: 44.6 us
  blocking collectives  21.6 us (48%)
  waiting for transfers between devices  9.48 us (21%)
  Pallas kernels  4.72 us (11%)
  starting transfers between devices  4.45 us (10%)
  local copies, waits for them, and re-layouts  1.92 us (4%)
  between operations  1.41 us (3%)
  matrix products  0.89 us (2%)
    all_to_all x1, blocking collectives, exchange(): lax.all_to_all(values, ('dp', 'tp'), 0, 0, tiled=True, axis_index_groups=...  21.6 us
    all_to_all x1, waiting for transfers between devices, exchange(): lax.all_to_all(values, ('dp', 'tp'), 0, 0, tiled=True, axis_index_groups=...  9.48 us
    all_to_all x1, starting transfers between devices, exchange(): lax.all_to_all(values, ('dp', 'tp'), 0, 0, tiled=True, axis_index_groups=...  4.45 us
    pallas_call x1, Pallas kernels, partial_sums(): pl.pallas_call(functools.partial(partial_kernel, TILE), out_shape=jax.Sha...  3.81 us
    unnamed x11, local copies, waits for them, and re-layouts  1.12 us
  transfers between devices with their start and end apart: 1, of which 1 were waited for; matrix products, arithmetic and copies ran while one was open for 6% of the time, Pallas kernels for 0%

profile of v4, /device:TPU:12, one launch (start us, length us, event | category | flops | bytes accessed | tf_op | source)
XLA Modules:
  0.0 44.6 jit_solution(3724074537418441181)
XLA Ops:
  0.6 3.8 %partial_sums.1 = bf16[256,3584]{1,0:T(8,128)(2,1)} custom-call(bf16[288,256]{1,0:T(8,128)(2,1)} %bitcast.25, bf16[288,3584]{1,0:T(8,128)(2,1)} %down_hbm.1), custom_call_target="tpu_custom_call" | custom-call | flops 528482304 | bytes 4046848 | tf_op jit(solution)/shard_map/partial_sums/pallas_call | solution.py:122
  4.4 0.0 copy-start
  4.5 0.0 copy-start.1
  4.5 0.0 copy-start.3
  4.5 0.0 copy-start.4
  4.5 0.0 copy-start.2
  4.5 4.5 %all-to-all-start = ((bf16[4,64,3584]{2,1,0:T(8,128)(2,1)}), bf16[4,64,3584]{2,1,0:T(8,128)(2,1)S(1)}, u32[]{:S(2)}, u32[]{:S(2)}) async-start(bf16[4,64,3584]{2,1,0:T(8,128)(2,1)} %bitcast.23), calls=%async_computation | async-start | bytes 3670016 | tf_op jit(solution)/shard_map/all_to_all | solution.py:193
  9.6 0.0 copy-done
  9.6 0.8 %reshape.83 = bf16[8,64,576]{2,1,0:T(8,128)(2,1)S(1)} reshape(bf16[8,36864]{1,0:T(8,128)(2,1)S(1)} %copy-done) | data formatting | bytes 1179648 | tf_op jit(solution)/shard_map/reshape | solution.py:24
  10.4 0.0 copy-done.1
  10.4 0.0 copy-done.3
  10.5 0.0 copy-done.4
  10.5 0.1 fusion.12
  10.6 0.0 copy-done.2
  10.6 0.5 %fusion.13 = (f32[8,64]{1,0:T(8,128)S(1)}, f32[8,64,256]{2,1,0:T(8,128)S(1)}) fusion(pred[8,256]{1,0:T(8,128)(4,1)S(1)} %fusion.12, bf16[8,64,576]{2,1,0:T(8,128)(2,1)S(1)} %reshape.83, bf16[256,576]{0,1:T(8,128)(2,1)S(1)} %copy-done.2), kind=kOutput, calls=%fused_computation.21 | convolution fusion | flops 151650560 | bytes 1413120 | tf_op jit(solution)/shard_map/sub | solution.py:36
  11.1 0.4 fusion.3
  11.5 1.1 %copy.12 = bf16[1,8,64,512]{3,1,2,0:T(8,128)(2,1)} copy(bf16[1,8,64,512]{3,2,1,0:T(8,128)(2,1)S(1)} %fusion.3) | data formatting | bytes 1048576
  12.6 9.5 %all-to-all-done = bf16[4,64,3584]{2,1,0:T(8,128)(2,1)S(1)} async-done(((bf16[4,64,3584]{2,1,0:T(8,128)(2,1)}), bf16[4,64,3584]{2,1,0:T(8,128)(2,1)S(1)}, u32[]{:S(2)}, u32[]{:S(2)}) %all-to-all-start) | async-done | bytes 1835040 | tf_op jit(solution)/shard_map/all_to_all | solution.py:193
  22.0 0.2 sum_parts.1
  22.3 21.6 %all_to_all.23 = bf16[8,8,3584]{2,1,0:T(8,128)(2,1)S(1)} all-to-all(bf16[8,8,3584]{2,1,0:T(8,128)(2,1)S(1)} %bitcast.22), channel_id=1, replica_groups={{9,1,12,4,14,6,15,7},{10,2,11,3,13,5,8,0},{17,25,20,28,22,30,23,31},{18..., dimensions={0} | all-to-all | bytes 917504 | tf_op jit(solution)/shard_map/all_to_all | solution.py:193
  43.9 0.7 %final_sum.1 = bf16[8,3584]{1,0:T(8,128)(2,1)} custom-call(s32[1]{0:T(128)} %copy.13.count_ref, bf16[64,3584]{1,0:T(8,128)(2,1)S(1)} %bitcast.21), custom_call_target="tpu_custom_call" | custom-call | tf_op jit(solution)/shard_map/final_sum/pallas_call | solution.py:182
  (3 shorter events, 0.0 us)
Async XLA Ops:
  4.4 5.2 %copy-start = (bf16[8,36864]{1,0:T(8,128)(2,1)S(1)}, bf16[8,36864]{1,0:T(8,128)(2,1)}, u32[]{:S(2)}) copy-start(bf16[8,36864]{1,0:T(8,128)(2,1)} %param.8) | copy-start | bytes 1769476
  4.5 6.0 %copy-start.1 = (s32[8]{0:T(128)S(1)}, s32[8]{0:T(128)}, u32[]{:S(2)}) copy-start(s32[8]{0:T(128)} %param.12) | copy-start | bytes 100
  4.5 6.0 %copy-start.3 = (s32[8]{0:T(128)S(1)}, s32[8]{0:T(128)}, u32[]{:S(2)}) copy-start(s32[8]{0:T(128)} %param.13) | copy-start | bytes 100
  4.5 6.0 %copy-start.4 = (s32[8]{0:T(128)S(1)}, s32[8]{0:T(128)}, u32[]{:S(2)}) copy-start(s32[8]{0:T(128)} %param.11) | copy-start | bytes 100
  4.5 6.1 %copy-start.2 = (bf16[256,576]{0,1:T(8,128)(2,1)S(1)}, bf16[256,576]{0,1:T(8,128)(2,1)}, u32[]{:S(2)}) copy-start(bf16[256,576]{0,1:T(8,128)(2,1)} %param.9) | copy-start | bytes 884740
  4.5 17.5 %all-to-all-start = ((bf16[4,64,3584]{2,1,0:T(8,128)(2,1)}), bf16[4,64,3584]{2,1,0:T(8,128)(2,1)S(1)}, u32[]{:S(2)}, u32[]{:S(2)}) async-start(bf16[4,64,3584]{2,1,0:T(8,128)(2,1)} %bitcast.23), calls=%async_computation | async-start | bytes 3670016 | tf_op jit(solution)/shard_map/all_to_all | solution.py:193

commit v5 on v3

v5 whole, which is shorter than its diff:
```python
import functools

import jax
import jax.numpy as jnp
from jax import lax
from jax.experimental import pallas as pl
from jax.experimental.pallas import tpu as pltpu
from jax.sharding import PartitionSpec as P

HEADS = 64
KVL = 512
QK_DIM = 192
LAT = 576
X_RING = 4
Y_RING = 8
TILE = 1792


def attend_local(queries, cache_latent, lengths, offsets, kinds, alive):
    row_total = queries.shape[0]
    entries = cache_latent.shape[0]
    scale = QK_DIM ** (-0.5)
    query_rows = queries.reshape(row_total, HEADS, LAT)
    scores = (
        jnp.einsum("rhd,kd->rhk", query_rows, cache_latent, preferred_element_type=jnp.float32)
        * scale
    )
    index = lax.broadcasted_iota(jnp.int32, (1, entries), 1)
    top_entry = (lengths + offsets)[:, None]
    causal = index <= top_entry
    verify = (index < lengths[:, None]) | (index == top_entry)
    allowed = jnp.where(kinds[:, None] == 1, verify, causal)[:, None, :]
    masked = jnp.where(allowed, scores, jnp.float32(-1e30))
    peak = jnp.max(masked, axis=-1, keepdims=True)
    expo = jnp.where(allowed, jnp.exp(masked - peak), jnp.float32(0.0))
    probs = (expo / jnp.sum(expo, axis=-1, keepdims=True)).astype(jnp.bfloat16)
    output = jnp.einsum(
        "rhk,kd->rhd", probs, cache_latent[:, :KVL], preferred_element_type=jnp.float32
    )
    output = jnp.where(alive[:, None, None], output, jnp.float32(0.0))
    return output.astype(jnp.bfloat16).reshape(row_total, HEADS * KVL)


FLIPS = (6, 12)


def member(block, kind):
    return 2 * block + ((kind ^ block) & 1)


def member_y(block, kind, core):
    flips = FLIPS[0] + core * (FLIPS[1] - FLIPS[0])
    return 2 * block + (kind ^ ((flips >> block) & 1))


def device(group, x, y):
    shift = 1 - group % 2
    return group * X_RING * Y_RING + (x + shift) % X_RING * Y_RING + (y + shift) % Y_RING


def flip_pairs(groups, flip):
    return [
        (device(g, x, y), device(g, x ^ (flip >> 1), y ^ (flip & 1)))
        for g in range(groups)
        for x in range(X_RING)
        for y in range(Y_RING)
    ]


def kind_groups(groups):
    return [
        [
            device(g, member(bx, sx), member_y(by, sy, g % 2))
            for by in range(Y_RING // 2)
            for bx in range(X_RING // 2)
        ]
        for g in range(groups)
        for sx in range(2)
        for sy in range(2)
    ]


def own_kind(core, place):
    shift = 1 - core
    x, y = ((place >> 3) - shift) & 3, (place - shift) & 7
    flips = FLIPS[0] + core * (FLIPS[1] - FLIPS[0])
    return 2 * ((x ^ (x >> 1)) & 1) + ((y ^ (flips >> (y >> 1))) & 1)


def row_order(index, core, kind):
    slot, block = index & 7, index >> 3
    to = (block >> 3) ^ kind
    sx, sy, by, bx = to >> 1, to & 1, (block >> 1) & 3, block & 1
    x, y, shift = member(bx, sx), member_y(by, sy, core), 1 - core
    return ((((x + shift) & 3) << 3) + ((y + shift) & 7)) * 8 + slot


def partial_kernel(tile, units_hbm, down_hbm, *refs):
    (units, down, out, in_sems, out_sems), outs_hbm = refs[-5:], refs[:-5]
    rows = outs_hbm[0].shape[0]
    tiles = down.shape[0]
    unit_copy = pltpu.make_async_copy(units_hbm, units, in_sems.at[tiles])
    unit_copy.start()
    copies = [
        pltpu.make_async_copy(down_hbm.at[:, pl.ds(j * tile, tile)], down.at[j], in_sems.at[j])
        for j in range(tiles)
    ]
    for copy in copies:
        copy.start()
    total = units.shape[1]
    core = lax.axis_index("dp") & 1
    kind = own_kind(core, lax.axis_index("tp"))
    order = row_order(lax.broadcasted_iota(jnp.int32, (total, total), 0), core, kind)
    pick = order == lax.broadcasted_iota(jnp.int32, (total, total), 1)
    pick = jnp.where(pick, 1.0, 0.0).astype(jnp.bfloat16)
    unit_copy.wait()
    ordered = lax.dot_general(
        pick, units[...], (((1,), (1,)), ((), ())), preferred_element_type=jnp.float32
    ).astype(jnp.bfloat16)
    sends = []
    for j, copy in enumerate(copies):
        copy.wait()
        out[j] = jnp.dot(ordered, down[j], preferred_element_type=jnp.float32).astype(jnp.bfloat16)
        for k, out_hbm in enumerate(outs_hbm):
            send = pltpu.make_async_copy(
                out.at[j, pl.ds(k * rows, rows)],
                out_hbm.at[:, pl.ds(j * tile, tile)],
                out_sems.at[j, k],
            )
            send.start()
            sends.append(send)
    for send in sends:
        send.wait()


def partial_sums(units_t, down_proj):
    units, total = units_t.shape
    width = down_proj.shape[1]
    tiles = width // TILE
    return pl.pallas_call(
        functools.partial(partial_kernel, TILE),
        out_shape=[jax.ShapeDtypeStruct((total // 4, width), jnp.bfloat16)] * 4,
        in_specs=[
            pl.BlockSpec(memory_space=pl.ANY),
            pl.BlockSpec(memory_space=pl.ANY),
        ],
        out_specs=[pl.BlockSpec(memory_space=pl.ANY)] * 4,
        scratch_shapes=[
            pltpu.VMEM((units, total), jnp.bfloat16),
            pltpu.VMEM((tiles, units, TILE), jnp.bfloat16),
            pltpu.VMEM((tiles, total, TILE), jnp.bfloat16),
            pltpu.SemaphoreType.DMA((tiles + 1,)),
            pltpu.SemaphoreType.DMA((tiles, 4)),
        ],
        compiler_params=pltpu.CompilerParams(vmem_limit_bytes=56 * 2**20),
        cost_estimate=pl.CostEstimate(
            flops=2 * total * units * width,
            bytes_accessed=2 * (units * (width + total) + total * width),
            transcendentals=0,
        ),
        name="partial_sums",
    )(units_t, down_proj)


def sum_kernel(*refs):
    value = refs[0][...].astype(jnp.float32)
    for ref in refs[1:-1]:
        value += ref[...].astype(jnp.float32)
    refs[-1][...] = value.astype(jnp.bfloat16)


def sum_arrays(*arrays):
    return pl.pallas_call(
        sum_kernel,
        out_shape=jax.ShapeDtypeStruct(arrays[0].shape, jnp.bfloat16),
        compiler_params=pltpu.CompilerParams(vmem_limit_bytes=16 * 2**20),
        name="sum_arrays",
    )(*arrays)


def final_kernel(count_ref, in_ref, out_ref):
    rows = out_ref.shape[0]
    value = jnp.zeros(out_ref.shape, jnp.float32)
    for pair in range(0, in_ref.shape[0], 2 * rows):
        both = in_ref[pl.ds(pair, 2 * rows), :].astype(jnp.float32)
        value += both[:rows] + both[rows:]
    row = lax.broadcasted_iota(jnp.int32, value.shape, 0)
    out_ref[...] = jnp.where(row < count_ref[0], value, 0.0).astype(jnp.bfloat16)


def final_sum(counts, values, rows):
    return pl.pallas_call(
        final_kernel,
        out_shape=jax.ShapeDtypeStruct((rows, values.shape[1]), jnp.bfloat16),
        in_specs=[
            pl.BlockSpec(memory_space=pltpu.SMEM),
            pl.BlockSpec(memory_space=pltpu.VMEM),
        ],
        compiler_params=pltpu.CompilerParams(vmem_limit_bytes=16 * 2**20),
        name="final_sum",
    )(counts, values)


def exchange(values, groups):
    return lax.all_to_all(values, ("dp", "tp"), 0, 0, tiled=True, axis_index_groups=groups)


def solution(mesh):
    groups = mesh.shape["dp"]

    def shards(
        queries, cache_latent, row_counts, row_kinds, cache_lengths, positions, hidden_units, down_proj
    ):
        row_total = queries.shape[0]
        alive = lax.broadcasted_iota(jnp.int32, (row_total,), 0) < row_counts[0]
        parts = list(partial_sums(hidden_units.T, down_proj))
        for flip in (3, 2, 1):
            parts[flip] = lax.ppermute(parts[flip], ("dp", "tp"), flip_pairs(groups, flip))
        attended = attend_local(queries, cache_latent, cache_lengths, positions, row_kinds, alive)
        quarter = sum_arrays(*(parts[flip] for flip in (0, 3, 2, 1)))
        quarter, attended = lax.optimization_barrier((quarter, attended))
        moved = exchange(quarter, kind_groups(groups))
        summed = final_sum(row_counts, moved, row_total)
        return (attended, summed)

    placed = (
        P(("dp", "tp"), None),
        P(("dp", "tp"), None),
        P(("dp", "tp")),
        P(("dp", "tp")),
        P(("dp", "tp")),
        P(("dp", "tp")),
        P("dp", "tp"),
        P("tp", None),
    )
    return jax.shard_map(
        shards,
        mesh=mesh,
        in_specs=placed,
        out_specs=(P(("dp", "tp"), None), P(("dp", "tp"), None)),
        check_vma=False,
    )
```

time: 46.5 us -> 45 us (0.968)
  waiting for transfers between devices: 9.43 us -> 4.61 us
  blocking collectives: 18.2 us -> 20.7 us
  starting transfers between devices: 9.52 us -> 10.4 us
    ppermute x0 -> x3, starting transfers between devices: none -> 10.4 us  [shards(): lax.ppermute(parts[flip], ('dp', 'tp'), flip_pairs(groups, flip))]
    all_to_all x1 -> x0, starting transfers between devices: 9.52 us -> none  [exchange(): lax.all_to_all(values, ('dp', 'tp'), 0, 0, tiled=True, axis_index_groups=...]
    all_to_all x1 -> x0, waiting for transfers between devices: 9.43 us -> none  [exchange(): lax.all_to_all(values, ('dp', 'tp'), 0, 0, tiled=True, axis_index_groups=...]
    ppermute x0 -> x3, waiting for transfers between devices: none -> 4.61 us  [shards(): lax.ppermute(parts[flip], ('dp', 'tp'), flip_pairs(groups, flip))]
    all_to_all x1, blocking collectives: 18.2 us -> 20.7 us  [exchange(): lax.all_to_all(values, ('dp', 'tp'), 0, 0, tiled=True, axis_index_groups=...]
    unnamed x11 -> x13, local copies, waits for them, and re-layouts: 1.12 us -> 1.11 us
  transfers between devices with their start and end apart: 1 -> 3, of which waited for: 1 -> 2; matrix products, arithmetic and copies ran while one was open for 6% -> 6% of each run, Pallas kernels for 0% -> 0%
where the time goes in v5:
time: 45 us; the launch traced here: 44.8 us
  blocking collectives  20.7 us (46%)
  starting transfers between devices  10.4 us (23%)
  Pallas kernels  4.74 us (11%)
  waiting for transfers between devices  4.61 us (10%)
  local copies, waits for them, and re-layouts  1.91 us (4%)
  between operations  1.44 us (3%)
  matrix products  0.89 us (2%)
    all_to_all x1, blocking collectives, exchange(): lax.all_to_all(values, ('dp', 'tp'), 0, 0, tiled=True, axis_index_groups=...  20.7 us
    ppermute x3, starting transfers between devices, shards(): lax.ppermute(parts[flip], ('dp', 'tp'), flip_pairs(groups, flip))  10.4 us
    ppermute x3, waiting for transfers between devices, shards(): lax.ppermute(parts[flip], ('dp', 'tp'), flip_pairs(groups, flip))  4.61 us
    pallas_call x1, Pallas kernels, partial_sums(): pl.pallas_call(functools.partial(partial_kernel, TILE), out_shape=[jax.Sh...  3.83 us
    unnamed x13, local copies, waits for them, and re-layouts  1.11 us
  transfers between devices with their start and end apart: 3, of which 2 were waited for; matrix products, arithmetic and copies ran while one was open for 6% of the time, Pallas kernels for 0%

profile of v5, /device:TPU:8, one launch (start us, length us, event | category | flops | bytes accessed | tf_op | source)
XLA Modules:
  0.0 44.8 jit_solution(13577374616253068655)
XLA Ops:
  0.6 0.0 copy-start.1
  0.6 0.0 copy-start.4
  0.7 0.0 copy-start.2
  0.7 0.0 copy-start.5
  0.7 0.0 copy-start.3
  0.7 3.8 %partial_sums.1 = (bf16[64,3584]{1,0:T(8,128)(2,1)}, bf16[64,3584]{1,0:T(8,128)(2,1)}, bf16[64,3584]{1,0:T(8,128)(2,1)}, bf16[64,3584]{1,0:T(8,128)(2,1)}) custom-call(bf16[288,256]{1,0:T(8,128)(2,1)} %bitcast.21, bf16[288,3584]{1,0:T(8,128)(2,1)} %down_hbm.1), custom_call_target="tpu_custom_call" | custom-call | flops 528482304 | bytes 4046848 | tf_op jit(solution)/shard_map/partial_sums/pallas_call | solution.py:140
  4.5 5.7 %collective-permute-start = (bf16[64,3584]{1,0:T(8,128)(2,1)}, bf16[64,3584]{1,0:T(8,128)(2,1)S(1)}, u32[]{:S(2)}, u32[]{:S(2)}) collective-permute-start(bf16[64,3584]{1,0:T(8,128)(2,1)} %get-tuple-element.9), channel_id=1, source_target_pairs={{9,18},{10,17},{11,20},{12,19},{13,22},{14,21},{15,16},{8,23},{17,... | collective-permute-start | bytes 1376264 | tf_op jit(solution)/shard_map/ppermute | solution.py:218
  10.2 2.4 %collective-permute-start.1 = (bf16[64,3584]{1,0:T(8,128)(2,1)}, bf16[64,3584]{1,0:T(8,128)(2,1)S(1)}, u32[]{:S(2)}, u32[]{:S(2)}) collective-permute-start(bf16[64,3584]{1,0:T(8,128)(2,1)} %get-tuple-element.10), channel_id=1, source_target_pairs={{9,17},{10,18},{11,19},{12,20},{13,21},{14,22},{15,23},{8,16},{17,... | collective-permute-start | bytes 1376264 | tf_op jit(solution)/shard_map/ppermute | solution.py:218
  12.6 2.4 %collective-permute-start.2 = (bf16[64,3584]{1,0:T(8,128)(2,1)}, bf16[64,3584]{1,0:T(8,128)(2,1)S(1)}, u32[]{:S(2)}, u32[]{:S(2)}) collective-permute-start(bf16[64,3584]{1,0:T(8,128)(2,1)} %get-tuple-element.11), channel_id=1, source_target_pairs={{9,10},{10,9},{11,12},{12,11},{13,14},{14,13},{15,8},{8,15},{17,18... | collective-permute-start | bytes 1376264 | tf_op jit(solution)/shard_map/ppermute | solution.py:218
  15.0 0.0 copy-done.1
  15.0 0.8 %reshape.81 = bf16[8,64,576]{2,1,0:T(8,128)(2,1)S(1)} reshape(bf16[8,36864]{1,0:T(8,128)(2,1)S(1)} %copy-done.1) | data formatting | bytes 1179648 | tf_op jit(solution)/shard_map/reshape | solution.py:23
  15.8 0.0 copy-done.4
  16.5 0.0 copy-done.2
  16.5 0.0 copy-done.5
  16.5 0.1 fusion.12
  16.6 0.0 copy-done.3
  16.6 0.5 %fusion.13 = (f32[8,64]{1,0:T(8,128)S(1)}, f32[8,64,256]{2,1,0:T(8,128)S(1)}) fusion(pred[8,256]{1,0:T(8,128)(4,1)S(1)} %fusion.12, bf16[8,64,576]{2,1,0:T(8,128)(2,1)S(1)} %reshape.81, bf16[256,576]{0,1:T(8,128)(2,1)S(1)} %copy-done.3), kind=kOutput, calls=%fused_computation.21 | convolution fusion | flops 151650560 | bytes 1413120 | tf_op jit(solution)/shard_map/sub | solution.py:35
  17.1 0.0 copy-start
  17.1 0.4 fusion.3
  17.5 1.1 %copy.12 = bf16[1,8,64,512]{3,1,2,0:T(8,128)(2,1)} copy(bf16[1,8,64,512]{3,2,1,0:T(8,128)(2,1)S(1)} %fusion.3) | data formatting | bytes 1048576
  18.6 0.0 collective-permute-done.refs_1_
  18.6 3.5 %collective-permute-done.1.refs_2_ = bf16[64,3584]{1,0:T(8,128)(2,1)S(1)} collective-permute-done((bf16[64,3584]{1,0:T(8,128)(2,1)}, bf16[64,3584]{1,0:T(8,128)(2,1)S(1)}, u32[]{:S(2)}, u32[]{:S(2)}) %collective-permute-start.1) | collective-permute-done | bytes 458784 | tf_op jit(solution)/shard_map/ppermute | solution.py:218
  22.1 1.1 %collective-permute-done.2.refs_3_ = bf16[64,3584]{1,0:T(8,128)(2,1)S(1)} collective-permute-done((bf16[64,3584]{1,0:T(8,128)(2,1)}, bf16[64,3584]{1,0:T(8,128)(2,1)S(1)}, u32[]{:S(2)}, u32[]{:S(2)}) %collective-permute-start.2) | collective-permute-done | bytes 458784 | tf_op jit(solution)/shard_map/ppermute | solution.py:218
  23.2 0.0 copy-done
  23.2 0.2 sum_arrays.1
  23.4 20.7 %all_to_all.11 = bf16[8,8,3584]{2,1,0:T(8,128)(2,1)S(1)} all-to-all(bf16[8,8,3584]{2,1,0:T(8,128)(2,1)S(1)} %bitcast.19), channel_id=1, replica_groups={{9,1,12,4,14,6,15,7},{10,2,11,3,13,5,8,0},{17,25,20,28,22,30,23,31},{18..., dimensions={0} | all-to-all | bytes 917504 | tf_op jit(solution)/shard_map/all_to_all | solution.py:205
  44.1 0.7 %final_sum.1 = bf16[8,3584]{1,0:T(8,128)(2,1)} custom-call(s32[1]{0:T(128)} %copy.13.count_ref, bf16[64,3584]{1,0:T(8,128)(2,1)S(1)} %bitcast.18), custom_call_target="tpu_custom_call" | custom-call | tf_op jit(solution)/shard_map/final_sum/pallas_call | solution.py:192
  (3 shorter events, 0.0 us)
Async XLA Ops:
  0.6 14.3 %copy-start.1 = (bf16[8,36864]{1,0:T(8,128)(2,1)S(1)}, bf16[8,36864]{1,0:T(8,128)(2,1)}, u32[]{:S(2)}) copy-start(bf16[8,36864]{1,0:T(8,128)(2,1)} %param.8) | copy-start | bytes 1769476
  0.6 15.1 %copy-start.4 = (s32[8]{0:T(128)S(1)}, s32[8]{0:T(128)}, u32[]{:S(2)}) copy-start(s32[8]{0:T(128)} %param.11) | copy-start | bytes 100
  0.7 15.8 %copy-start.2 = (s32[8]{0:T(128)S(1)}, s32[8]{0:T(128)}, u32[]{:S(2)}) copy-start(s32[8]{0:T(128)} %param.12) | copy-start | bytes 100
  0.7 15.8 %copy-start.5 = (s32[8]{0:T(128)S(1)}, s32[8]{0:T(128)}, u32[]{:S(2)}) copy-start(s32[8]{0:T(128)} %param.13) | copy-start | bytes 100
  0.7 15.9 %copy-start.3 = (bf16[256,576]{0,1:T(8,128)(2,1)S(1)}, bf16[256,576]{0,1:T(8,128)(2,1)}, u32[]{:S(2)}) copy-start(bf16[256,576]{0,1:T(8,128)(2,1)} %param.9) | copy-start | bytes 884740
  4.5 14.1 %collective-permute-start = (bf16[64,3584]{1,0:T(8,128)(2,1)}, bf16[64,3584]{1,0:T(8,128)(2,1)S(1)}, u32[]{:S(2)}, u32[]{:S(2)}) collective-permute-start(bf16[64,3584]{1,0:T(8,128)(2,1)} %get-tuple-element.9), channel_id=1, source_target_pairs={{9,18},{10,17},{11,20},{12,19},{13,22},{14,21},{15,16},{8,23},{17,... | collective-permute-start | bytes 1376264 | tf_op jit(solution)/shard_map/ppermute | solution.py:218
  10.2 11.9 %collective-permute-start.1 = (bf16[64,3584]{1,0:T(8,128)(2,1)}, bf16[64,3584]{1,0:T(8,128)(2,1)S(1)}, u32[]{:S(2)}, u32[]{:S(2)}) collective-permute-start(bf16[64,3584]{1,0:T(8,128)(2,1)} %get-tuple-element.10), channel_id=1, source_target_pairs={{9,17},{10,18},{11,19},{12,20},{13,21},{14,22},{15,23},{8,16},{17,... | collective-permute-start | bytes 1376264 | tf_op jit(solution)/shard_map/ppermute | solution.py:218
  12.6 10.6 %collective-permute-start.2 = (bf16[64,3584]{1,0:T(8,128)(2,1)}, bf16[64,3584]{1,0:T(8,128)(2,1)S(1)}, u32[]{:S(2)}, u32[]{:S(2)}) collective-permute-start(bf16[64,3584]{1,0:T(8,128)(2,1)} %get-tuple-element.11), channel_id=1, source_target_pairs={{9,10},{10,9},{11,12},{12,11},{13,14},{14,13},{15,8},{8,15},{17,18... | collective-permute-start | bytes 1376264 | tf_op jit(solution)/shard_map/ppermute | solution.py:218
  17.1 6.1 %copy-start = (bf16[64,3584]{1,0:T(8,128)(2,1)S(1)}, bf16[64,3584]{1,0:T(8,128)(2,1)}, u32[]{:S(2)}) copy-start(bf16[64,3584]{1,0:T(8,128)(2,1)} %get-tuple-element.8.refs_0_) | copy-start | bytes 1376260

commit v6 on v5

--- a/solution.py
+++ b/solution.py
@@ -41,16 +41,15 @@
     return output.astype(jnp.bfloat16).reshape(row_total, HEADS * KVL)
 
 
-FLIPS = (6, 12)
+FLIPS = 6
 
 
 def member(block, kind):
     return 2 * block + ((kind ^ block) & 1)
 
 
-def member_y(block, kind, core):
-    flips = FLIPS[0] + core * (FLIPS[1] - FLIPS[0])
-    return 2 * block + (kind ^ ((flips >> block) & 1))
+def member_y(block, kind):
+    return 2 * block + (kind ^ ((FLIPS >> block) & 1))
 
 
 def device(group, x, y):
@@ -70,7 +69,7 @@
 def kind_groups(groups):
     return [
         [
-            device(g, member(bx, sx), member_y(by, sy, g % 2))
+            device(g, member(bx, sx), member_y(by, sy))
             for by in range(Y_RING // 2)
             for bx in range(X_RING // 2)
         ]
@@ -83,15 +82,14 @@
 def own_kind(core, place):
     shift = 1 - core
     x, y = ((place >> 3) - shift) & 3, (place - shift) & 7
-    flips = FLIPS[0] + core * (FLIPS[1] - FLIPS[0])
-    return 2 * ((x ^ (x >> 1)) & 1) + ((y ^ (flips >> (y >> 1))) & 1)
+    return 2 * ((x ^ (x >> 1)) & 1) + ((y ^ (FLIPS >> (y >> 1))) & 1)
 
 
 def row_order(index, core, kind):
     slot, block = index & 7, index >> 3
     to = (block >> 3) ^ kind
     sx, sy, by, bx = to >> 1, to & 1, (block >> 1) & 3, block & 1
-    x, y, shift = member(bx, sx), member_y(by, sy, core), 1 - core
+    x, y, shift = member(bx, sx), member_y(by, sy), 1 - core
     return ((((x + shift) & 3) << 3) + ((y + shift) & 7)) * 8 + slot
 
 

time: 45 us -> 44.3 us (0.984)
  blocking collectives: 20.7 us -> 19.9 us
    all_to_all x1, blocking collectives: 20.7 us -> 19.9 us  [exchange(): lax.all_to_all(values, ('dp', 'tp'), 0, 0, tiled=True, axis_index_groups=...]
  transfers between devices with their start and end apart: 3 -> 3, of which waited for: 2 -> 2; matrix products, arithmetic and copies ran while one was open for 6% -> 7% of each run, Pallas kernels for 0% -> 0%
where the time goes in v6:
time: 44.3 us; the launch traced here: 44 us
  blocking collectives  19.9 us (45%)
  starting transfers between devices  10.4 us (23%)
  Pallas kernels  4.74 us (11%)
  waiting for transfers between devices  4.61 us (10%)
  local copies, waits for them, and re-layouts  1.91 us (4%)
  between operations  1.44 us (3%)
  matrix products  0.89 us (2%)
    all_to_all x1, blocking collectives, exchange(): lax.all_to_all(values, ('dp', 'tp'), 0, 0, tiled=True, axis_index_groups=...  19.9 us
    ppermute x3, starting transfers between devices, shards(): lax.ppermute(parts[flip], ('dp', 'tp'), flip_pairs(groups, flip))  10.4 us
    ppermute x3, waiting for transfers between devices, shards(): lax.ppermute(parts[flip], ('dp', 'tp'), flip_pairs(groups, flip))  4.61 us
    pallas_call x1, Pallas kernels, partial_sums(): pl.pallas_call(functools.partial(partial_kernel, TILE), out_shape=[jax.Sh...  3.83 us
    unnamed x13, local copies, waits for them, and re-layouts  1.11 us
  transfers between devices with their start and end apart: 3, of which 2 were waited for; matrix products, arithmetic and copies ran while one was open for 7% of the time, Pallas kernels for 0%

profile of v6, /device:TPU:8, one launch (start us, length us, event | category | flops | bytes accessed | tf_op | source)
XLA Modules:
  0.0 44.0 jit_solution(13462241870998090009)
XLA Ops:
  0.6 0.0 copy-start.1
  0.6 0.0 copy-start.4
  0.7 0.0 copy-start.2
  0.7 0.0 copy-start.5
  0.7 0.0 copy-start.3
  0.7 3.8 %partial_sums.1 = (bf16[64,3584]{1,0:T(8,128)(2,1)}, bf16[64,3584]{1,0:T(8,128)(2,1)}, bf16[64,3584]{1,0:T(8,128)(2,1)}, bf16[64,3584]{1,0:T(8,128)(2,1)}) custom-call(bf16[288,256]{1,0:T(8,128)(2,1)} %bitcast.21, bf16[288,3584]{1,0:T(8,128)(2,1)} %down_hbm.1), custom_call_target="tpu_custom_call" | custom-call | flops 528482304 | bytes 4046848 | tf_op jit(solution)/shard_map/partial_sums/pallas_call | solution.py:138
  4.5 5.7 %collective-permute-start = (bf16[64,3584]{1,0:T(8,128)(2,1)}, bf16[64,3584]{1,0:T(8,128)(2,1)S(1)}, u32[]{:S(2)}, u32[]{:S(2)}) collective-permute-start(bf16[64,3584]{1,0:T(8,128)(2,1)} %get-tuple-element.9), channel_id=1, source_target_pairs={{9,18},{10,17},{11,20},{12,19},{13,22},{14,21},{15,16},{8,23},{17,... | collective-permute-start | bytes 1376264 | tf_op jit(solution)/shard_map/ppermute | solution.py:216
  10.2 2.4 %collective-permute-start.1 = (bf16[64,3584]{1,0:T(8,128)(2,1)}, bf16[64,3584]{1,0:T(8,128)(2,1)S(1)}, u32[]{:S(2)}, u32[]{:S(2)}) collective-permute-start(bf16[64,3584]{1,0:T(8,128)(2,1)} %get-tuple-element.10), channel_id=1, source_target_pairs={{9,17},{10,18},{11,19},{12,20},{13,21},{14,22},{15,23},{8,16},{17,... | collective-permute-start | bytes 1376264 | tf_op jit(solution)/shard_map/ppermute | solution.py:216
  12.6 2.4 %collective-permute-start.2 = (bf16[64,3584]{1,0:T(8,128)(2,1)}, bf16[64,3584]{1,0:T(8,128)(2,1)S(1)}, u32[]{:S(2)}, u32[]{:S(2)}) collective-permute-start(bf16[64,3584]{1,0:T(8,128)(2,1)} %get-tuple-element.11), channel_id=1, source_target_pairs={{9,10},{10,9},{11,12},{12,11},{13,14},{14,13},{15,8},{8,15},{17,18... | collective-permute-start | bytes 1376264 | tf_op jit(solution)/shard_map/ppermute | solution.py:216
  15.0 0.0 copy-done.1
  15.0 0.8 %reshape.81 = bf16[8,64,576]{2,1,0:T(8,128)(2,1)S(1)} reshape(bf16[8,36864]{1,0:T(8,128)(2,1)S(1)} %copy-done.1) | data formatting | bytes 1179648 | tf_op jit(solution)/shard_map/reshape | solution.py:23
  15.8 0.0 copy-done.4
  16.5 0.0 copy-done.2
  16.5 0.0 copy-done.5
  16.5 0.1 fusion.12
  16.6 0.0 copy-done.3
  16.6 0.5 %fusion.13 = (f32[8,64]{1,0:T(8,128)S(1)}, f32[8,64,256]{2,1,0:T(8,128)S(1)}) fusion(pred[8,256]{1,0:T(8,128)(4,1)S(1)} %fusion.12, bf16[8,64,576]{2,1,0:T(8,128)(2,1)S(1)} %reshape.81, bf16[256,576]{0,1:T(8,128)(2,1)S(1)} %copy-done.3), kind=kOutput, calls=%fused_computation.21 | convolution fusion | flops 151650560 | bytes 1413120 | tf_op jit(solution)/shard_map/sub | solution.py:35
  17.1 0.0 copy-start
  17.1 0.4 fusion.3
  17.5 1.1 %copy.12 = bf16[1,8,64,512]{3,1,2,0:T(8,128)(2,1)} copy(bf16[1,8,64,512]{3,2,1,0:T(8,128)(2,1)S(1)} %fusion.3) | data formatting | bytes 1048576
  18.6 0.0 collective-permute-done.refs_1_
  18.6 3.5 %collective-permute-done.1.refs_2_ = bf16[64,3584]{1,0:T(8,128)(2,1)S(1)} collective-permute-done((bf16[64,3584]{1,0:T(8,128)(2,1)}, bf16[64,3584]{1,0:T(8,128)(2,1)S(1)}, u32[]{:S(2)}, u32[]{:S(2)}) %collective-permute-start.1) | collective-permute-done | bytes 458784 | tf_op jit(solution)/shard_map/ppermute | solution.py:216
  22.1 1.1 %collective-permute-done.2.refs_3_ = bf16[64,3584]{1,0:T(8,128)(2,1)S(1)} collective-permute-done((bf16[64,3584]{1,0:T(8,128)(2,1)}, bf16[64,3584]{1,0:T(8,128)(2,1)S(1)}, u32[]{:S(2)}, u32[]{:S(2)}) %collective-permute-start.2) | collective-permute-done | bytes 458784 | tf_op jit(solution)/shard_map/ppermute | solution.py:216
  23.2 0.0 copy-done
  23.2 0.2 sum_arrays.1
  23.4 19.9 %all_to_all.11 = bf16[8,8,3584]{2,1,0:T(8,128)(2,1)S(1)} all-to-all(bf16[8,8,3584]{2,1,0:T(8,128)(2,1)S(1)} %bitcast.19), channel_id=1, replica_groups={{9,1,12,4,14,6,15,7},{10,2,11,3,13,5,8,0},{17,25,20,28,22,30,23,31},{18..., dimensions={0} | all-to-all | bytes 917504 | tf_op jit(solution)/shard_map/all_to_all | solution.py:203
  43.3 0.7 %final_sum.1 = bf16[8,3584]{1,0:T(8,128)(2,1)} custom-call(s32[1]{0:T(128)} %copy.13.count_ref, bf16[64,3584]{1,0:T(8,128)(2,1)S(1)} %bitcast.18), custom_call_target="tpu_custom_call" | custom-call | tf_op jit(solution)/shard_map/final_sum/pallas_call | solution.py:190
  (3 shorter events, 0.0 us)
Async XLA Ops:
  0.6 14.3 %copy-start.1 = (bf16[8,36864]{1,0:T(8,128)(2,1)S(1)}, bf16[8,36864]{1,0:T(8,128)(2,1)}, u32[]{:S(2)}) copy-start(bf16[8,36864]{1,0:T(8,128)(2,1)} %param.8) | copy-start | bytes 1769476
  0.6 15.1 %copy-start.4 = (s32[8]{0:T(128)S(1)}, s32[8]{0:T(128)}, u32[]{:S(2)}) copy-start(s32[8]{0:T(128)} %param.11) | copy-start | bytes 100
  0.7 15.8 %copy-start.2 = (s32[8]{0:T(128)S(1)}, s32[8]{0:T(128)}, u32[]{:S(2)}) copy-start(s32[8]{0:T(128)} %param.12) | copy-start | bytes 100
  0.7 15.8 %copy-start.5 = (s32[8]{0:T(128)S(1)}, s32[8]{0:T(128)}, u32[]{:S(2)}) copy-start(s32[8]{0:T(128)} %param.13) | copy-start | bytes 100
  0.7 15.9 %copy-start.3 = (bf16[256,576]{0,1:T(8,128)(2,1)S(1)}, bf16[256,576]{0,1:T(8,128)(2,1)}, u32[]{:S(2)}) copy-start(bf16[256,576]{0,1:T(8,128)(2,1)} %param.9) | copy-start | bytes 884740
  4.5 14.1 %collective-permute-start = (bf16[64,3584]{1,0:T(8,128)(2,1)}, bf16[64,3584]{1,0:T(8,128)(2,1)S(1)}, u32[]{:S(2)}, u32[]{:S(2)}) collective-permute-start(bf16[64,3584]{1,0:T(8,128)(2,1)} %get-tuple-element.9), channel_id=1, source_target_pairs={{9,18},{10,17},{11,20},{12,19},{13,22},{14,21},{15,16},{8,23},{17,... | collective-permute-start | bytes 1376264 | tf_op jit(solution)/shard_map/ppermute | solution.py:216
  10.2 11.9 %collective-permute-start.1 = (bf16[64,3584]{1,0:T(8,128)(2,1)}, bf16[64,3584]{1,0:T(8,128)(2,1)S(1)}, u32[]{:S(2)}, u32[]{:S(2)}) collective-permute-start(bf16[64,3584]{1,0:T(8,128)(2,1)} %get-tuple-element.10), channel_id=1, source_target_pairs={{9,17},{10,18},{11,19},{12,20},{13,21},{14,22},{15,23},{8,16},{17,... | collective-permute-start | bytes 1376264 | tf_op jit(solution)/shard_map/ppermute | solution.py:216
  12.6 10.6 %collective-permute-start.2 = (bf16[64,3584]{1,0:T(8,128)(2,1)}, bf16[64,3584]{1,0:T(8,128)(2,1)S(1)}, u32[]{:S(2)}, u32[]{:S(2)}) collective-permute-start(bf16[64,3584]{1,0:T(8,128)(2,1)} %get-tuple-element.11), channel_id=1, source_target_pairs={{9,10},{10,9},{11,12},{12,11},{13,14},{14,13},{15,8},{8,15},{17,18... | collective-permute-start | bytes 1376264 | tf_op jit(solution)/shard_map/ppermute | solution.py:216
  17.1 6.1 %copy-start = (bf16[64,3584]{1,0:T(8,128)(2,1)S(1)}, bf16[64,3584]{1,0:T(8,128)(2,1)}, u32[]{:S(2)}) copy-start(bf16[64,3584]{1,0:T(8,128)(2,1)} %get-tuple-element.8.refs_0_) | copy-start | bytes 1376260

commit v7 on v6

--- a/solution.py
+++ b/solution.py
@@ -70,8 +70,7 @@
     return [
         [
             device(g, member(bx, sx), member_y(by, sy))
-            for by in range(Y_RING // 2)
-            for bx in range(X_RING // 2)
+            for by, bx in ((0, 0), (0, 1), (1, 1), (1, 0), (2, 0), (2, 1), (3, 1), (3, 0))
         ]
         for g in range(groups)
         for sx in range(2)
@@ -88,7 +87,7 @@
 def row_order(index, core, kind):
     slot, block = index & 7, index >> 3
     to = (block >> 3) ^ kind
-    sx, sy, by, bx = to >> 1, to & 1, (block >> 1) & 3, block & 1
+    sx, sy, by, bx = to >> 1, to & 1, (64080 >> (2 * (block & 7))) & 3, (102 >> (block & 7)) & 1
     x, y, shift = member(bx, sx), member_y(by, sy), 1 - core
     return ((((x + shift) & 3) << 3) + ((y + shift) & 7)) * 8 + slot
 

time: 44.3 us -> 44 us (level)
  no operation moved by 1% of the time
where the time goes in v7:
time: 44 us; the launch traced here: 43.7 us
  blocking collectives  19.6 us (45%)
  starting transfers between devices  10.4 us (24%)
  Pallas kernels  4.74 us (11%)
  waiting for transfers between devices  4.61 us (10%)
  local copies, waits for them, and re-layouts  1.91 us (4%)
  between operations  1.44 us (3%)
  matrix products  0.89 us (2%)
    all_to_all x1, blocking collectives, exchange(): lax.all_to_all(values, ('dp', 'tp'), 0, 0, tiled=True, axis_index_groups=...  19.6 us
    ppermute x3, starting transfers between devices, shards(): lax.ppermute(parts[flip], ('dp', 'tp'), flip_pairs(groups, flip))  10.4 us
    ppermute x3, waiting for transfers between devices, shards(): lax.ppermute(parts[flip], ('dp', 'tp'), flip_pairs(groups, flip))  4.61 us
    pallas_call x1, Pallas kernels, partial_sums(): pl.pallas_call(functools.partial(partial_kernel, TILE), out_shape=[jax.Sh...  3.83 us
    unnamed x13, local copies, waits for them, and re-layouts  1.11 us
  transfers between devices with their start and end apart: 3, of which 2 were waited for; matrix products, arithmetic and copies ran while one was open for 7% of the time, Pallas kernels for 0%

profile of v7, /device:TPU:8, one launch (start us, length us, event | category | flops | bytes accessed | tf_op | source)
XLA Modules:
  0.0 43.7 jit_solution(13505740372646557292)
XLA Ops:
  0.6 0.0 copy-start.1
  0.6 0.0 copy-start.4
  0.7 0.0 copy-start.2
  0.7 0.0 copy-start.5
  0.7 0.0 copy-start.3
  0.7 3.8 %partial_sums.1 = (bf16[64,3584]{1,0:T(8,128)(2,1)}, bf16[64,3584]{1,0:T(8,128)(2,1)}, bf16[64,3584]{1,0:T(8,128)(2,1)}, bf16[64,3584]{1,0:T(8,128)(2,1)}) custom-call(bf16[288,256]{1,0:T(8,128)(2,1)} %bitcast.21, bf16[288,3584]{1,0:T(8,128)(2,1)} %down_hbm.1), custom_call_target="tpu_custom_call" | custom-call | flops 528482304 | bytes 4046848 | tf_op jit(solution)/shard_map/partial_sums/pallas_call | solution.py:137
  4.5 5.7 %collective-permute-start = (bf16[64,3584]{1,0:T(8,128)(2,1)}, bf16[64,3584]{1,0:T(8,128)(2,1)S(1)}, u32[]{:S(2)}, u32[]{:S(2)}) collective-permute-start(bf16[64,3584]{1,0:T(8,128)(2,1)} %get-tuple-element.9), channel_id=1, source_target_pairs={{9,18},{10,17},{11,20},{12,19},{13,22},{14,21},{15,16},{8,23},{17,... | collective-permute-start | bytes 1376264 | tf_op jit(solution)/shard_map/ppermute | solution.py:215
  10.2 2.4 %collective-permute-start.1 = (bf16[64,3584]{1,0:T(8,128)(2,1)}, bf16[64,3584]{1,0:T(8,128)(2,1)S(1)}, u32[]{:S(2)}, u32[]{:S(2)}) collective-permute-start(bf16[64,3584]{1,0:T(8,128)(2,1)} %get-tuple-element.10), channel_id=1, source_target_pairs={{9,17},{10,18},{11,19},{12,20},{13,21},{14,22},{15,23},{8,16},{17,... | collective-permute-start | bytes 1376264 | tf_op jit(solution)/shard_map/ppermute | solution.py:215
  12.6 2.4 %collective-permute-start.2 = (bf16[64,3584]{1,0:T(8,128)(2,1)}, bf16[64,3584]{1,0:T(8,128)(2,1)S(1)}, u32[]{:S(2)}, u32[]{:S(2)}) collective-permute-start(bf16[64,3584]{1,0:T(8,128)(2,1)} %get-tuple-element.11), channel_id=1, source_target_pairs={{9,10},{10,9},{11,12},{12,11},{13,14},{14,13},{15,8},{8,15},{17,18... | collective-permute-start | bytes 1376264 | tf_op jit(solution)/shard_map/ppermute | solution.py:215
  15.0 0.0 copy-done.1
  15.0 0.8 %reshape.81 = bf16[8,64,576]{2,1,0:T(8,128)(2,1)S(1)} reshape(bf16[8,36864]{1,0:T(8,128)(2,1)S(1)} %copy-done.1) | data formatting | bytes 1179648 | tf_op jit(solution)/shard_map/reshape | solution.py:23
  15.8 0.0 copy-done.4
  16.5 0.0 copy-done.2
  16.5 0.0 copy-done.5
  16.5 0.1 fusion.12
  16.6 0.0 copy-done.3
  16.6 0.5 %fusion.13 = (f32[8,64]{1,0:T(8,128)S(1)}, f32[8,64,256]{2,1,0:T(8,128)S(1)}) fusion(pred[8,256]{1,0:T(8,128)(4,1)S(1)} %fusion.12, bf16[8,64,576]{2,1,0:T(8,128)(2,1)S(1)} %reshape.81, bf16[256,576]{0,1:T(8,128)(2,1)S(1)} %copy-done.3), kind=kOutput, calls=%fused_computation.21 | convolution fusion | flops 151650560 | bytes 1413120 | tf_op jit(solution)/shard_map/sub | solution.py:35
  17.1 0.0 copy-start
  17.1 0.4 fusion.3
  17.5 1.1 %copy.12 = bf16[1,8,64,512]{3,1,2,0:T(8,128)(2,1)} copy(bf16[1,8,64,512]{3,2,1,0:T(8,128)(2,1)S(1)} %fusion.3) | data formatting | bytes 1048576
  18.6 0.0 collective-permute-done.refs_1_
  18.6 3.5 %collective-permute-done.1.refs_2_ = bf16[64,3584]{1,0:T(8,128)(2,1)S(1)} collective-permute-done((bf16[64,3584]{1,0:T(8,128)(2,1)}, bf16[64,3584]{1,0:T(8,128)(2,1)S(1)}, u32[]{:S(2)}, u32[]{:S(2)}) %collective-permute-start.1) | collective-permute-done | bytes 458784 | tf_op jit(solution)/shard_map/ppermute | solution.py:215
  22.1 1.1 %collective-permute-done.2.refs_3_ = bf16[64,3584]{1,0:T(8,128)(2,1)S(1)} collective-permute-done((bf16[64,3584]{1,0:T(8,128)(2,1)}, bf16[64,3584]{1,0:T(8,128)(2,1)S(1)}, u32[]{:S(2)}, u32[]{:S(2)}) %collective-permute-start.2) | collective-permute-done | bytes 458784 | tf_op jit(solution)/shard_map/ppermute | solution.py:215
  23.2 0.0 copy-done
  23.2 0.2 sum_arrays.1
  23.4 19.6 %all_to_all.11 = bf16[8,8,3584]{2,1,0:T(8,128)(2,1)S(1)} all-to-all(bf16[8,8,3584]{2,1,0:T(8,128)(2,1)S(1)} %bitcast.19), channel_id=1, replica_groups={{9,1,4,12,14,6,7,15},{10,2,3,11,13,5,0,8},{17,25,28,20,22,30,31,23},{18..., dimensions={0} | all-to-all | bytes 917504 | tf_op jit(solution)/shard_map/all_to_all | solution.py:202
  43.0 0.7 %final_sum.1 = bf16[8,3584]{1,0:T(8,128)(2,1)} custom-call(s32[1]{0:T(128)} %copy.13.count_ref, bf16[64,3584]{1,0:T(8,128)(2,1)S(1)} %bitcast.18), custom_call_target="tpu_custom_call" | custom-call | tf_op jit(solution)/shard_map/final_sum/pallas_call | solution.py:189
  (3 shorter events, 0.0 us)
Async XLA Ops:
  0.6 14.3 %copy-start.1 = (bf16[8,36864]{1,0:T(8,128)(2,1)S(1)}, bf16[8,36864]{1,0:T(8,128)(2,1)}, u32[]{:S(2)}) copy-start(bf16[8,36864]{1,0:T(8,128)(2,1)} %param.8) | copy-start | bytes 1769476
  0.6 15.1 %copy-start.4 = (s32[8]{0:T(128)S(1)}, s32[8]{0:T(128)}, u32[]{:S(2)}) copy-start(s32[8]{0:T(128)} %param.11) | copy-start | bytes 100
  0.7 15.8 %copy-start.2 = (s32[8]{0:T(128)S(1)}, s32[8]{0:T(128)}, u32[]{:S(2)}) copy-start(s32[8]{0:T(128)} %param.12) | copy-start | bytes 100
  0.7 15.8 %copy-start.5 = (s32[8]{0:T(128)S(1)}, s32[8]{0:T(128)}, u32[]{:S(2)}) copy-start(s32[8]{0:T(128)} %param.13) | copy-start | bytes 100
  0.7 15.9 %copy-start.3 = (bf16[256,576]{0,1:T(8,128)(2,1)S(1)}, bf16[256,576]{0,1:T(8,128)(2,1)}, u32[]{:S(2)}) copy-start(bf16[256,576]{0,1:T(8,128)(2,1)} %param.9) | copy-start | bytes 884740
  4.5 14.1 %collective-permute-start = (bf16[64,3584]{1,0:T(8,128)(2,1)}, bf16[64,3584]{1,0:T(8,128)(2,1)S(1)}, u32[]{:S(2)}, u32[]{:S(2)}) collective-permute-start(bf16[64,3584]{1,0:T(8,128)(2,1)} %get-tuple-element.9), channel_id=1, source_target_pairs={{9,18},{10,17},{11,20},{12,19},{13,22},{14,21},{15,16},{8,23},{17,... | collective-permute-start | bytes 1376264 | tf_op jit(solution)/shard_map/ppermute | solution.py:215
  10.2 11.9 %collective-permute-start.1 = (bf16[64,3584]{1,0:T(8,128)(2,1)}, bf16[64,3584]{1,0:T(8,128)(2,1)S(1)}, u32[]{:S(2)}, u32[]{:S(2)}) collective-permute-start(bf16[64,3584]{1,0:T(8,128)(2,1)} %get-tuple-element.10), channel_id=1, source_target_pairs={{9,17},{10,18},{11,19},{12,20},{13,21},{14,22},{15,23},{8,16},{17,... | collective-permute-start | bytes 1376264 | tf_op jit(solution)/shard_map/ppermute | solution.py:215
  12.6 10.6 %collective-permute-start.2 = (bf16[64,3584]{1,0:T(8,128)(2,1)}, bf16[64,3584]{1,0:T(8,128)(2,1)S(1)}, u32[]{:S(2)}, u32[]{:S(2)}) collective-permute-start(bf16[64,3584]{1,0:T(8,128)(2,1)} %get-tuple-element.11), channel_id=1, source_target_pairs={{9,10},{10,9},{11,12},{12,11},{13,14},{14,13},{15,8},{8,15},{17,18... | collective-permute-start | bytes 1376264 | tf_op jit(solution)/shard_map/ppermute | solution.py:215
  17.1 6.1 %copy-start = (bf16[64,3584]{1,0:T(8,128)(2,1)S(1)}, bf16[64,3584]{1,0:T(8,128)(2,1)}, u32[]{:S(2)}) copy-start(bf16[64,3584]{1,0:T(8,128)(2,1)} %get-tuple-element.8.refs_0_) | copy-start | bytes 1376260

commit v8 on v7

--- a/solution.py
+++ b/solution.py
@@ -214,7 +214,7 @@
         for flip in (3, 2, 1):
             parts[flip] = lax.ppermute(parts[flip], ("dp", "tp"), flip_pairs(groups, flip))
         attended = attend_local(queries, cache_latent, cache_lengths, positions, row_kinds, alive)
-        quarter = sum_arrays(*(parts[flip] for flip in (0, 3, 2, 1)))
+        quarter = sum_arrays(*(parts[flip] for flip in (0, 3, 1, 2)))
         quarter, attended = lax.optimization_barrier((quarter, attended))
         moved = exchange(quarter, kind_groups(groups))
         summed = final_sum(row_counts, moved, row_total)

time: 44 us -> 43.9 us (level)
  blocking collectives: 19.6 us -> 18.4 us
  waiting for transfers between devices: 4.61 us -> 5.79 us
    all_to_all x1, blocking collectives: 19.6 us -> 18.4 us  [exchange(): lax.all_to_all(values, ('dp', 'tp'), 0, 0, tiled=True, axis_index_groups=...]
    ppermute x3, waiting for transfers between devices: 4.61 us -> 5.79 us  [shards(): lax.ppermute(parts[flip], ('dp', 'tp'), flip_pairs(groups, flip))]
where the time goes in v8:
time: 43.9 us; the launch traced here: 43.7 us
  blocking collectives  18.4 us (42%)
  starting transfers between devices  10.4 us (24%)
  waiting for transfers between devices  5.79 us (13%)
  Pallas kernels  4.74 us (11%)
  local copies, waits for them, and re-layouts  1.91 us (4%)
  between operations  1.44 us (3%)
  matrix products  0.89 us (2%)
    all_to_all x1, blocking collectives, exchange(): lax.all_to_all(values, ('dp', 'tp'), 0, 0, tiled=True, axis_index_groups=...  18.4 us
    ppermute x3, starting transfers between devices, shards(): lax.ppermute(parts[flip], ('dp', 'tp'), flip_pairs(groups, flip))  10.4 us
    ppermute x3, waiting for transfers between devices, shards(): lax.ppermute(parts[flip], ('dp', 'tp'), flip_pairs(groups, flip))  5.79 us
    pallas_call x1, Pallas kernels, partial_sums(): pl.pallas_call(functools.partial(partial_kernel, TILE), out_shape=[jax.Sh...  3.83 us
    unnamed x13, local copies, waits for them, and re-layouts  1.11 us
  transfers between devices with their start and end apart: 3, of which 2 were waited for; matrix products, arithmetic and copies ran while one was open for 7% of the time, Pallas kernels for 0%

profile of v8, /device:TPU:8, one launch (start us, length us, event | category | flops | bytes accessed | tf_op | source)
XLA Modules:
  0.0 43.7 jit_solution(8010696594672641564)
XLA Ops:
  0.6 0.0 copy-start.1
  0.6 0.0 copy-start.4
  0.7 0.0 copy-start.2
  0.7 0.0 copy-start.5
  0.7 0.0 copy-start.3
  0.7 3.8 %partial_sums.1 = (bf16[64,3584]{1,0:T(8,128)(2,1)}, bf16[64,3584]{1,0:T(8,128)(2,1)}, bf16[64,3584]{1,0:T(8,128)(2,1)}, bf16[64,3584]{1,0:T(8,128)(2,1)}) custom-call(bf16[288,256]{1,0:T(8,128)(2,1)} %bitcast.21, bf16[288,3584]{1,0:T(8,128)(2,1)} %down_hbm.1), custom_call_target="tpu_custom_call" | custom-call | flops 528482304 | bytes 4046848 | tf_op jit(solution)/shard_map/partial_sums/pallas_call | solution.py:137
  4.5 5.7 %collective-permute-start = (bf16[64,3584]{1,0:T(8,128)(2,1)}, bf16[64,3584]{1,0:T(8,128)(2,1)S(1)}, u32[]{:S(2)}, u32[]{:S(2)}) collective-permute-start(bf16[64,3584]{1,0:T(8,128)(2,1)} %get-tuple-element.9), channel_id=1, source_target_pairs={{9,18},{10,17},{11,20},{12,19},{13,22},{14,21},{15,16},{8,23},{17,... | collective-permute-start | bytes 1376264 | tf_op jit(solution)/shard_map/ppermute | solution.py:215
  10.2 2.4 %collective-permute-start.1 = (bf16[64,3584]{1,0:T(8,128)(2,1)}, bf16[64,3584]{1,0:T(8,128)(2,1)S(1)}, u32[]{:S(2)}, u32[]{:S(2)}) collective-permute-start(bf16[64,3584]{1,0:T(8,128)(2,1)} %get-tuple-element.10), channel_id=1, source_target_pairs={{9,10},{10,9},{11,12},{12,11},{13,14},{14,13},{15,8},{8,15},{17,18... | collective-permute-start | bytes 1376264 | tf_op jit(solution)/shard_map/ppermute | solution.py:215
  12.6 2.4 %collective-permute-start.2 = (bf16[64,3584]{1,0:T(8,128)(2,1)}, bf16[64,3584]{1,0:T(8,128)(2,1)S(1)}, u32[]{:S(2)}, u32[]{:S(2)}) collective-permute-start(bf16[64,3584]{1,0:T(8,128)(2,1)} %get-tuple-element.11), channel_id=1, source_target_pairs={{9,17},{10,18},{11,19},{12,20},{13,21},{14,22},{15,23},{8,16},{17,... | collective-permute-start | bytes 1376264 | tf_op jit(solution)/shard_map/ppermute | solution.py:215
  15.0 0.0 copy-done.1
  15.0 0.8 %reshape.81 = bf16[8,64,576]{2,1,0:T(8,128)(2,1)S(1)} reshape(bf16[8,36864]{1,0:T(8,128)(2,1)S(1)} %copy-done.1) | data formatting | bytes 1179648 | tf_op jit(solution)/shard_map/reshape | solution.py:23
  15.8 0.0 copy-done.4
  16.5 0.0 copy-done.2
  16.5 0.0 copy-done.5
  16.5 0.1 fusion.12
  16.6 0.0 copy-done.3
  16.6 0.5 %fusion.13 = (f32[8,64]{1,0:T(8,128)S(1)}, f32[8,64,256]{2,1,0:T(8,128)S(1)}) fusion(pred[8,256]{1,0:T(8,128)(4,1)S(1)} %fusion.12, bf16[8,64,576]{2,1,0:T(8,128)(2,1)S(1)} %reshape.81, bf16[256,576]{0,1:T(8,128)(2,1)S(1)} %copy-done.3), kind=kOutput, calls=%fused_computation.21 | convolution fusion | flops 151650560 | bytes 1413120 | tf_op jit(solution)/shard_map/sub | solution.py:35
  17.1 0.0 copy-start
  17.1 0.4 fusion.3
  17.5 1.1 %copy.12 = bf16[1,8,64,512]{3,1,2,0:T(8,128)(2,1)} copy(bf16[1,8,64,512]{3,2,1,0:T(8,128)(2,1)S(1)} %fusion.3) | data formatting | bytes 1048576
  18.6 0.0 collective-permute-done.refs_1_
  18.6 3.6 %collective-permute-done.1.refs_2_ = bf16[64,3584]{1,0:T(8,128)(2,1)S(1)} collective-permute-done((bf16[64,3584]{1,0:T(8,128)(2,1)}, bf16[64,3584]{1,0:T(8,128)(2,1)S(1)}, u32[]{:S(2)}, u32[]{:S(2)}) %collective-permute-start.1) | collective-permute-done | bytes 458784 | tf_op jit(solution)/shard_map/ppermute | solution.py:215
  22.2 2.2 %collective-permute-done.2.refs_3_ = bf16[64,3584]{1,0:T(8,128)(2,1)S(1)} collective-permute-done((bf16[64,3584]{1,0:T(8,128)(2,1)}, bf16[64,3584]{1,0:T(8,128)(2,1)S(1)}, u32[]{:S(2)}, u32[]{:S(2)}) %collective-permute-start.2) | collective-permute-done | bytes 458784 | tf_op jit(solution)/shard_map/ppermute | solution.py:215
  24.4 0.0 copy-done
  24.4 0.2 sum_arrays.1
  24.6 18.4 %all_to_all.11 = bf16[8,8,3584]{2,1,0:T(8,128)(2,1)S(1)} all-to-all(bf16[8,8,3584]{2,1,0:T(8,128)(2,1)S(1)} %bitcast.19), channel_id=1, replica_groups={{9,1,4,12,14,6,7,15},{10,2,3,11,13,5,0,8},{17,25,28,20,22,30,31,23},{18..., dimensions={0} | all-to-all | bytes 917504 | tf_op jit(solution)/shard_map/all_to_all | solution.py:202
  43.0 0.7 %final_sum.1 = bf16[8,3584]{1,0:T(8,128)(2,1)} custom-call(s32[1]{0:T(128)} %copy.13.count_ref, bf16[64,3584]{1,0:T(8,128)(2,1)S(1)} %bitcast.18), custom_call_target="tpu_custom_call" | custom-call | tf_op jit(solution)/shard_map/final_sum/pallas_call | solution.py:189
  (3 shorter events, 0.0 us)
Async XLA Ops:
  0.6 14.3 %copy-start.1 = (bf16[8,36864]{1,0:T(8,128)(2,1)S(1)}, bf16[8,36864]{1,0:T(8,128)(2,1)}, u32[]{:S(2)}) copy-start(bf16[8,36864]{1,0:T(8,128)(2,1)} %param.8) | copy-start | bytes 1769476
  0.6 15.1 %copy-start.4 = (s32[8]{0:T(128)S(1)}, s32[8]{0:T(128)}, u32[]{:S(2)}) copy-start(s32[8]{0:T(128)} %param.11) | copy-start | bytes 100
  0.7 15.8 %copy-start.2 = (s32[8]{0:T(128)S(1)}, s32[8]{0:T(128)}, u32[]{:S(2)}) copy-start(s32[8]{0:T(128)} %param.12) | copy-start | bytes 100
  0.7 15.8 %copy-start.5 = (s32[8]{0:T(128)S(1)}, s32[8]{0:T(128)}, u32[]{:S(2)}) copy-start(s32[8]{0:T(128)} %param.13) | copy-start | bytes 100
  0.7 15.9 %copy-start.3 = (bf16[256,576]{0,1:T(8,128)(2,1)S(1)}, bf16[256,576]{0,1:T(8,128)(2,1)}, u32[]{:S(2)}) copy-start(bf16[256,576]{0,1:T(8,128)(2,1)} %param.9) | copy-start | bytes 884740
  4.5 14.1 %collective-permute-start = (bf16[64,3584]{1,0:T(8,128)(2,1)}, bf16[64,3584]{1,0:T(8,128)(2,1)S(1)}, u32[]{:S(2)}, u32[]{:S(2)}) collective-permute-start(bf16[64,3584]{1,0:T(8,128)(2,1)} %get-tuple-element.9), channel_id=1, source_target_pairs={{9,18},{10,17},{11,20},{12,19},{13,22},{14,21},{15,16},{8,23},{17,... | collective-permute-start | bytes 1376264 | tf_op jit(solution)/shard_map/ppermute | solution.py:215
  10.2 12.0 %collective-permute-start.1 = (bf16[64,3584]{1,0:T(8,128)(2,1)}, bf16[64,3584]{1,0:T(8,128)(2,1)S(1)}, u32[]{:S(2)}, u32[]{:S(2)}) collective-permute-start(bf16[64,3584]{1,0:T(8,128)(2,1)} %get-tuple-element.10), channel_id=1, source_target_pairs={{9,10},{10,9},{11,12},{12,11},{13,14},{14,13},{15,8},{8,15},{17,18... | collective-permute-start | bytes 1376264 | tf_op jit(solution)/shard_map/ppermute | solution.py:215
  12.6 11.8 %collective-permute-start.2 = (bf16[64,3584]{1,0:T(8,128)(2,1)}, bf16[64,3584]{1,0:T(8,128)(2,1)S(1)}, u32[]{:S(2)}, u32[]{:S(2)}) collective-permute-start(bf16[64,3584]{1,0:T(8,128)(2,1)} %get-tuple-element.11), channel_id=1, source_target_pairs={{9,17},{10,18},{11,19},{12,20},{13,21},{14,22},{15,23},{8,16},{17,... | collective-permute-start | bytes 1376264 | tf_op jit(solution)/shard_map/ppermute | solution.py:215
  17.1 7.2 %copy-start = (bf16[64,3584]{1,0:T(8,128)(2,1)S(1)}, bf16[64,3584]{1,0:T(8,128)(2,1)}, u32[]{:S(2)}) copy-start(bf16[64,3584]{1,0:T(8,128)(2,1)} %get-tuple-element.8.refs_0_) | copy-start | bytes 1376260
